TPU v7x, 32 devices: a whole 2x2x4 slice. The times are simulated.
32 devices in a mesh: member: 2 (over x), wide: 16 (over z, y, core).
Axes of the slice: x: 2, y: 2, z: 4, core: 2. Of those that a mesh axis runs over, the one named last changes fastest.
Arguments:
- stream_now: float32 [4, 256, 4096], P('member', 'wide'), parts along dimension 0, may hold values from -6 to 6
- vorticity: float32 [4, 256, 4096], P('member', 'wide'), parts along dimension 0, may hold values from -0.62 to 0.62
Outputs:
- vorticity_next: float32 [4, 256, 4096], P('member', 'wide'), parts along dimension 0
- stream_next: float32 [4, 256, 4096], P('member', 'wide'), parts along dimension 0
There are 2 independent parts, one for each index of `member`. A program takes and returns all parts, laid end to end along the dimension named above; each array names one. Nothing has to cross between parts.
All inputs are finite; a program needn't handle non-finite values.
Results may differ from a plain program's by a relative error of at most 0.00002.
Values sent between devices are 32-bit elements; how exact they have to be, the bound alone decides.
A program may use at most 128 MiB of HBM per device.

v0:
```python
import jax
import jax.numpy as jnp
from jax import lax
from jax.sharding import PartitionSpec as P

LEVELS = 5
SWEEPS = 2
COARSE_SWEEPS = 8


relax_weight = 0.8
coupling_upper = 0.02
coupling_lower = 0.04
time_step = 0.5
beta_slope = 0.05
bottom_drag = 0.02


def extended(cells, sides, width):
    for axis, dim in sides:
        count = lax.axis_size(axis)
        ends = count - 1
        head = lax.slice_in_dim(cells, 0, width, axis=dim)
        tail = lax.slice_in_dim(cells, cells.shape[dim] - width, cells.shape[dim], axis=dim)
        cells = jnp.concatenate(
            [
                lax.ppermute(tail, axis, [(i, (i + 1) % count) for i in range(ends)]),
                cells,
                lax.ppermute(head, axis, [((i + 1) % count, i) for i in range(ends)]),
            ],
            axis=dim,
        )
    return cells


def coupling():
    return jnp.array([coupling_upper, coupling_lower], jnp.float32)[:, None, None]


def diagonal(spacing):
    return 4.0 / (spacing * spacing) + coupling()


def neighbours(padded):
    interior = padded[:, 1:-1, :]
    return (
        padded[:, 2:, :]
        + padded[:, :-2, :]
        + jnp.roll(interior, 1, axis=2)
        + jnp.roll(interior, -1, axis=2)
    )


def apply_operator(padded, spacing):
    interior = padded[:, 1:-1, :]
    return (4.0 * interior - neighbours(padded)) / (spacing * spacing) + coupling() * (
        interior - interior[::-1]
    )


def jacobi(padded, source, spacing):
    return padded[:, 1:-1, :] + relax_weight * (
        source - apply_operator(padded, spacing)
    ) / diagonal(spacing)


def shifted(padded, row_step, col_step):
    row_count = padded.shape[1] - 2
    return jnp.roll(padded[:, 1 + row_step : 1 + row_step + row_count, :], -col_step, axis=2)


def arakawa(stream_padded, vorticity_padded):

    def stream_at(row_step, col_step):
        return shifted(stream_padded, row_step, col_step)

    def vorticity_at(row_step, col_step):
        return shifted(vorticity_padded, row_step, col_step)

    first_form = (stream_at(0, 1) - stream_at(0, -1)) * (
        vorticity_at(1, 0) - vorticity_at(-1, 0)
    ) - (stream_at(1, 0) - stream_at(-1, 0)) * (vorticity_at(0, 1) - vorticity_at(0, -1))
    second_form = (
        stream_at(0, 1) * (vorticity_at(1, 1) - vorticity_at(-1, 1))
        - stream_at(0, -1) * (vorticity_at(1, -1) - vorticity_at(-1, -1))
        - stream_at(1, 0) * (vorticity_at(1, 1) - vorticity_at(1, -1))
        + stream_at(-1, 0) * (vorticity_at(-1, 1) - vorticity_at(-1, -1))
    )
    third_form = (
        vorticity_at(1, 0) * (stream_at(1, 1) - stream_at(1, -1))
        - vorticity_at(-1, 0) * (stream_at(-1, 1) - stream_at(-1, -1))
        - vorticity_at(0, 1) * (stream_at(1, 1) - stream_at(-1, 1))
        + vorticity_at(0, -1) * (stream_at(1, -1) - stream_at(-1, -1))
    )
    return (first_form + second_form + third_form) / 12.0


def advance(stream_padded, vorticity_padded, stream_now, vorticity):
    jacobian = arakawa(stream_padded, vorticity_padded)
    zonal_slope = (jnp.roll(stream_now, -1, axis=2) - jnp.roll(stream_now, 1, axis=2)) * 0.5
    drag_term = jnp.array([0.0, bottom_drag], jnp.float32)[:, None, None] * (
        neighbours(stream_padded) - 4.0 * stream_now
    )
    return vorticity - time_step * (jacobian + beta_slope * zonal_slope + drag_term)


def restrict(residual):
    return 0.25 * (
        residual[:, 0::2, 0::2]
        + residual[:, 1::2, 0::2]
        + residual[:, 0::2, 1::2]
        + residual[:, 1::2, 1::2]
    )


def prolong(correction):
    layers, row_count, col_count = correction.shape
    spread = jnp.broadcast_to(correction[:, :, None, :, None], (layers, row_count, 2, col_count, 2))
    return spread.reshape(layers, 2 * row_count, 2 * col_count)


def sweep_rims(iterate):
    return extended(iterate, (("wide", 1),), 1)


def relax(iterate, source, spacing, zero_start, with_residual):
    for sweep_index in range(SWEEPS):
        if zero_start and sweep_index == 0:
            iterate = relax_weight * source / diagonal(spacing)
        else:
            iterate = jacobi(sweep_rims(iterate), source, spacing)
    if with_residual:
        residual = source - apply_operator(sweep_rims(iterate), spacing)
        return (iterate, residual)
    return (iterate, source)


def coarse_solve(source, spacing):
    iterate = relax_weight * source / diagonal(spacing)
    for sweep_index in range(1, COARSE_SWEEPS):
        padded = extended(iterate, (("wide", 1),), 1)
        iterate = jacobi(padded, source, spacing)
    return iterate


def vcycle(grid_level, iterate, source, zero_start):
    spacing = 2.0**grid_level
    if grid_level == LEVELS - 1:
        return coarse_solve(source, spacing)
    iterate, residual = relax(iterate, source, spacing, zero_start, True)
    coarse_source = restrict(residual)
    correction = vcycle(grid_level + 1, jnp.zeros_like(coarse_source), coarse_source, True)
    iterate = iterate + prolong(correction)
    iterate, ignored = relax(iterate, source, spacing, False, False)
    return iterate


def shards(stream_now, vorticity):
    stacked = extended(jnp.stack([stream_now, vorticity]), (("wide", 2),), 1)
    vorticity_next = advance(stacked[0], stacked[1], stream_now, vorticity)
    stream_next = vcycle(0, stream_now, -vorticity_next, False)
    return (vorticity_next, stream_next)


def solution(mesh):
    return jax.shard_map(
        shards,
        mesh=mesh,
        in_specs=(P("member", "wide", None), P("member", "wide", None)),
        out_specs=(P("member", "wide", None), P("member", "wide", None)),
        check_vma=False,
    )
```

profile of v0, /device:TPU:8, one launch (start us, length us, event | category | flops | bytes accessed | tf_op | source)
XLA Modules:
  0.0 307.8 jit_solution(18191690101724934882)
XLA Ops:
  1.8 2.8 collective-permute-start.2
  7.8 2.7 collective-permute-start
  10.5 3.8 %collective-permute-start.1 = (f32[2,2,1,4096]{3,2,1,0:T(1,128)S(1)}, f32[2,2,1,4096]{3,2,1,0:T(1,128)S(1)}, u32[]{:S(2)}, u32[]{:S(2)}) collective-permute-start(f32[2,2,1,4096]{3,2,1,0:T(1,128)S(1)} %get-tuple-element.15), channel_id=1, source_target_pairs={{1,0},{2,1},{3,2},{4,3},{5,4},{6,5},{7,6},{8,7},{9,8},{10,9},{11,1... | collective-permute-start | bytes 196616 | tf_op jit(solution)/shard_map/ppermute | solution.py:29
  20.0 4.6 %collective-permute-start.4 = (f32[2,1,4096]{2,1,0:T(1,128)S(1)}, f32[2,1,4096]{2,1,0:T(1,128)S(1)}, u32[]{:S(2)}, u32[]{:S(2)}) collective-permute-start(f32[2,1,4096]{2,1,0:T(1,128)S(1)} %get-tuple-element.62), channel_id=1, source_target_pairs={{1,0},{2,1},{3,2},{4,3},{5,4},{6,5},{7,6},{8,7},{9,8},{10,9},{11,1... | collective-permute-start | bytes 98312 | tf_op jit(solution)/shard_map/ppermute | solution.py:29
  26.6 4.1 %collective-permute-done.5 = f32[2,1,4096]{2,1,0:T(1,128)S(1)} collective-permute-done((f32[2,1,4096]{2,1,0:T(1,128)S(1)}, f32[2,1,4096]{2,1,0:T(1,128)S(1)}, u32[]{:S(2)}, u32[]{:S(2)}) %collective-permute-start.5) | collective-permute-done | bytes 32800 | tf_op jit(solution)/shard_map/ppermute | solution.py:27
  33.3 2.9 collective-permute-start.7
  36.3 3.2 %collective-permute-done.7 = f32[2,1,4096]{2,1,0:T(1,128)S(1)} collective-permute-done((f32[2,1,4096]{2,1,0:T(1,128)S(1)}, f32[2,1,4096]{2,1,0:T(1,128)S(1)}, u32[]{:S(2)}, u32[]{:S(2)}) %collective-permute-start.7) | collective-permute-done | bytes 32800 | tf_op jit(solution)/shard_map/ppermute | solution.py:27
  39.9 4.4 %slice.840 = f32[2,8,2048]{2,1,0:T(8,128)S(1)} slice(f32[2,16,4096]{2,1,0:T(8,128)S(1)} %fusion.14), slice={[0:2:1], [1:16:2], [1:4096:2]} | slice | bytes 262144 | tf_op jit(solution)/shard_map/slice | solution.py:112
  44.3 4.4 %slice.839 = f32[2,8,2048]{2,1,0:T(8,128)S(1)} slice(f32[2,16,4096]{2,1,0:T(8,128)S(1)} %fusion.14), slice={[0:2:1], [0:16:2], [1:4096:2]} | slice | bytes 262144 | tf_op jit(solution)/shard_map/slice | solution.py:111
  48.7 4.6 %slice.838 = f32[2,8,2048]{2,1,0:T(8,128)S(1)} slice(f32[2,16,4096]{2,1,0:T(8,128)S(1)} %fusion.14), slice={[0:2:1], [1:16:2], [0:4096:2]} | slice | bytes 262144 | tf_op jit(solution)/shard_map/slice | solution.py:110
  53.2 4.4 %slice.837 = f32[2,8,2048]{2,1,0:T(8,128)S(1)} slice(f32[2,16,4096]{2,1,0:T(8,128)S(1)} %fusion.14), slice={[0:2:1], [0:16:2], [0:4096:2]} | slice | bytes 262144 | tf_op jit(solution)/shard_map/slice | solution.py:109
  59.8 2.4 collective-permute-start.9
  62.3 3.5 %collective-permute-done.9 = f32[2,1,2048]{2,1,0:T(1,128)S(1)} collective-permute-done((f32[2,1,2048]{2,1,0:T(1,128)S(1)}, f32[2,1,2048]{2,1,0:T(1,128)S(1)}, u32[]{:S(2)}, u32[]{:S(2)}) %collective-permute-start.9) | collective-permute-done | bytes 16416 | tf_op jit(solution)/shard_map/ppermute | solution.py:27
  68.0 2.4 collective-permute-start.11
  70.5 3.5 %collective-permute-done.11 = f32[2,1,2048]{2,1,0:T(1,128)S(1)} collective-permute-done((f32[2,1,2048]{2,1,0:T(1,128)S(1)}, f32[2,1,2048]{2,1,0:T(1,128)S(1)}, u32[]{:S(2)}, u32[]{:S(2)}) %collective-permute-start.11) | collective-permute-done | bytes 16416 | tf_op jit(solution)/shard_map/ppermute | solution.py:27
  80.8 2.4 collective-permute-start.13
  83.3 3.4 %collective-permute-done.13 = f32[2,1,1024]{2,1,0:T(1,128)S(1)} collective-permute-done((f32[2,1,1024]{2,1,0:T(1,128)S(1)}, f32[2,1,1024]{2,1,0:T(1,128)S(1)}, u32[]{:S(2)}, u32[]{:S(2)}) %collective-permute-start.13) | collective-permute-done | bytes 8224 | tf_op jit(solution)/shard_map/ppermute | solution.py:27
  88.8 2.6 collective-permute-start.15
  91.5 3.2 %collective-permute-done.15 = f32[2,1,1024]{2,1,0:T(1,128)S(1)} collective-permute-done((f32[2,1,1024]{2,1,0:T(1,128)S(1)}, f32[2,1,1024]{2,1,0:T(1,128)S(1)}, u32[]{:S(2)}, u32[]{:S(2)}) %collective-permute-start.15) | collective-permute-done | bytes 8224 | tf_op jit(solution)/shard_map/ppermute | solution.py:27
  98.4 2.4 collective-permute-start.17
  100.9 3.3 %collective-permute-done.17 = f32[2,1,512]{2,1,0:T(1,128)S(1)} collective-permute-done((f32[2,1,512]{2,1,0:T(1,128)S(1)}, f32[2,1,512]{2,1,0:T(1,128)S(1)}, u32[]{:S(2)}, u32[]{:S(2)}) %collective-permute-start.17) | collective-permute-done | bytes 4128 | tf_op jit(solution)/shard_map/ppermute | solution.py:27
  108.8 3.3 %collective-permute-done.19 = f32[2,1,512]{2,1,0:T(1,128)S(1)} collective-permute-done((f32[2,1,512]{2,1,0:T(1,128)S(1)}, f32[2,1,512]{2,1,0:T(1,128)S(1)}, u32[]{:S(2)}, u32[]{:S(2)}) %collective-permute-start.19) | collective-permute-done | bytes 4128 | tf_op jit(solution)/shard_map/ppermute | solution.py:27
  115.2 4.5 %collective-permute-start.20 = (f32[2,1,256]{2,1,0:T(1,128)S(1)}, f32[2,1,256]{2,1,0:T(1,128)S(1)}, u32[]{:S(2)}, u32[]{:S(2)}) collective-permute-start(f32[2,1,256]{2,1,0:T(1,128)S(1)} %get-tuple-element.2), channel_id=1, source_target_pairs={{1,0},{2,1},{3,2},{4,3},{5,4},{6,5},{7,6},{8,7},{9,8},{10,9},{11,1... | collective-permute-start | bytes 6152 | tf_op jit(solution)/shard_map/ppermute | solution.py:29
  123.1 4.5 %collective-permute-start.22 = (f32[2,1,256]{2,1,0:T(1,128)S(1)}, f32[2,1,256]{2,1,0:T(1,128)S(1)}, u32[]{:S(2)}, u32[]{:S(2)}) collective-permute-start(f32[2,1,256]{2,1,0:T(1,128)S(1)} %multiply_add_fusion.9), channel_id=1, source_target_pairs={{1,0},{2,1},{3,2},{4,3},{5,4},{6,5},{7,6},{8,7},{9,8},{10,9},{11,1... | collective-permute-start | bytes 6152 | tf_op jit(solution)/shard_map/ppermute | solution.py:29
  129.1 2.4 collective-permute-start.25
  131.6 4.0 %collective-permute-start.24 = (f32[2,1,256]{2,1,0:T(1,128)S(1)}, f32[2,1,256]{2,1,0:T(1,128)S(1)}, u32[]{:S(2)}, u32[]{:S(2)}) collective-permute-start(f32[2,1,256]{2,1,0:T(1,128)S(1)} %multiply_add_fusion.8), channel_id=1, source_target_pairs={{1,0},{2,1},{3,2},{4,3},{5,4},{6,5},{7,6},{8,7},{9,8},{10,9},{11,1... | collective-permute-start | bytes 6152 | tf_op jit(solution)/shard_map/ppermute | solution.py:29
  137.0 2.4 collective-permute-start.27
  139.5 4.0 %collective-permute-start.26 = (f32[2,1,256]{2,1,0:T(1,128)S(1)}, f32[2,1,256]{2,1,0:T(1,128)S(1)}, u32[]{:S(2)}, u32[]{:S(2)}) collective-permute-start(f32[2,1,256]{2,1,0:T(1,128)S(1)} %multiply_add_fusion.7), channel_id=1, source_target_pairs={{1,0},{2,1},{3,2},{4,3},{5,4},{6,5},{7,6},{8,7},{9,8},{10,9},{11,1... | collective-permute-start | bytes 6152 | tf_op jit(solution)/shard_map/ppermute | solution.py:29
  144.9 2.4 collective-permute-start.29
  147.4 4.0 %collective-permute-start.28 = (f32[2,1,256]{2,1,0:T(1,128)S(1)}, f32[2,1,256]{2,1,0:T(1,128)S(1)}, u32[]{:S(2)}, u32[]{:S(2)}) collective-permute-start(f32[2,1,256]{2,1,0:T(1,128)S(1)} %multiply_add_fusion.6), channel_id=1, source_target_pairs={{1,0},{2,1},{3,2},{4,3},{5,4},{6,5},{7,6},{8,7},{9,8},{10,9},{11,1... | collective-permute-start | bytes 6152 | tf_op jit(solution)/shard_map/ppermute | solution.py:29
  152.9 2.4 collective-permute-start.31
  155.3 4.0 %collective-permute-start.30 = (f32[2,1,256]{2,1,0:T(1,128)S(1)}, f32[2,1,256]{2,1,0:T(1,128)S(1)}, u32[]{:S(2)}, u32[]{:S(2)}) collective-permute-start(f32[2,1,256]{2,1,0:T(1,128)S(1)} %multiply_add_fusion.5), channel_id=1, source_target_pairs={{1,0},{2,1},{3,2},{4,3},{5,4},{6,5},{7,6},{8,7},{9,8},{10,9},{11,1... | collective-permute-start | bytes 6152 | tf_op jit(solution)/shard_map/ppermute | solution.py:29
  160.8 2.4 collective-permute-start.33
  163.2 4.0 %collective-permute-start.32 = (f32[2,1,256]{2,1,0:T(1,128)S(1)}, f32[2,1,256]{2,1,0:T(1,128)S(1)}, u32[]{:S(2)}, u32[]{:S(2)}) collective-permute-start(f32[2,1,256]{2,1,0:T(1,128)S(1)} %multiply_add_fusion.4), channel_id=1, source_target_pairs={{1,0},{2,1},{3,2},{4,3},{5,4},{6,5},{7,6},{8,7},{9,8},{10,9},{11,1... | collective-permute-start | bytes 6152 | tf_op jit(solution)/shard_map/ppermute | solution.py:29
  169.1 4.5 %collective-permute-start.34 = (f32[2,1,512]{2,1,0:T(1,128)S(1)}, f32[2,1,512]{2,1,0:T(1,128)S(1)}, u32[]{:S(2)}, u32[]{:S(2)}) collective-permute-start(f32[2,1,512]{2,1,0:T(1,128)S(1)} %get-tuple-element.124), channel_id=1, source_target_pairs={{1,0},{2,1},{3,2},{4,3},{5,4},{6,5},{7,6},{8,7},{9,8},{10,9},{11,1... | collective-permute-start | bytes 12296 | tf_op jit(solution)/shard_map/ppermute | solution.py:29
  175.6 3.8 %collective-permute-done.35 = f32[2,1,512]{2,1,0:T(1,128)S(1)} collective-permute-done((f32[2,1,512]{2,1,0:T(1,128)S(1)}, f32[2,1,512]{2,1,0:T(1,128)S(1)}, u32[]{:S(2)}, u32[]{:S(2)}) %collective-permute-start.35) | collective-permute-done | bytes 4128 | tf_op jit(solution)/shard_map/ppermute | solution.py:27
  184.0 3.3 %collective-permute-done.37 = f32[2,1,512]{2,1,0:T(1,128)S(1)} collective-permute-done((f32[2,1,512]{2,1,0:T(1,128)S(1)}, f32[2,1,512]{2,1,0:T(1,128)S(1)}, u32[]{:S(2)}, u32[]{:S(2)}) %collective-permute-start.37) | collective-permute-done | bytes 4128 | tf_op jit(solution)/shard_map/ppermute | solution.py:27
  193.5 3.4 %collective-permute-done.39 = f32[2,1,1024]{2,1,0:T(1,128)S(1)} collective-permute-done((f32[2,1,1024]{2,1,0:T(1,128)S(1)}, f32[2,1,1024]{2,1,0:T(1,128)S(1)}, u32[]{:S(2)}, u32[]{:S(2)}) %collective-permute-start.39) | collective-permute-done | bytes 8224 | tf_op jit(solution)/shard_map/ppermute | solution.py:27
  201.5 3.4 %collective-permute-done.41 = f32[2,1,1024]{2,1,0:T(1,128)S(1)} collective-permute-done((f32[2,1,1024]{2,1,0:T(1,128)S(1)}, f32[2,1,1024]{2,1,0:T(1,128)S(1)}, u32[]{:S(2)}, u32[]{:S(2)}) %collective-permute-start.41) | collective-permute-done | bytes 8224 | tf_op jit(solution)/shard_map/ppermute | solution.py:27
  205.0 4.0 %broadcast_in_dim.19 = f32[2,4,2,1024,2]{4,3,2,1,0:T(8,128)} broadcast(f32[2,4,1024]{2,1,0:T(4,128)S(1)} %fusion.108), dimensions={0,1,3} | broadcast | bytes 163840 | tf_op jit(solution)/shard_map/broadcast_in_dim | solution.py:118
  209.0 8.7 %reshape.125 = f32[2,8,2048]{2,1,0:T(8,128)S(1)} reshape(f32[2,4,2,1024,2]{4,3,2,1,0:T(8,128)} %broadcast_in_dim.19) | data formatting | bytes 262144 | tf_op jit(solution)/shard_map/reshape | solution.py:119
  222.3 3.5 %collective-permute-done.43 = f32[2,1,2048]{2,1,0:T(1,128)S(1)} collective-permute-done((f32[2,1,2048]{2,1,0:T(1,128)S(1)}, f32[2,1,2048]{2,1,0:T(1,128)S(1)}, u32[]{:S(2)}, u32[]{:S(2)}) %collective-permute-start.43) | collective-permute-done | bytes 16416 | tf_op jit(solution)/shard_map/ppermute | solution.py:27
  228.0 2.7 collective-permute-start.45
  230.7 3.2 %collective-permute-done.45 = f32[2,1,2048]{2,1,0:T(1,128)S(1)} collective-permute-done((f32[2,1,2048]{2,1,0:T(1,128)S(1)}, f32[2,1,2048]{2,1,0:T(1,128)S(1)}, u32[]{:S(2)}, u32[]{:S(2)}) %collective-permute-start.45) | collective-permute-done | bytes 16416 | tf_op jit(solution)/shard_map/ppermute | solution.py:27
  234.1 11.4 %broadcast_in_dim.20 = f32[2,8,2,2048,2]{4,3,2,1,0:T(8,128)} broadcast(f32[2,8,2048]{2,1,0:T(8,128)S(1)} %fusion.67), dimensions={0,1,3} | broadcast | bytes 655360 | tf_op jit(solution)/shard_map/broadcast_in_dim | solution.py:118
  245.4 43.6 %reshape.126 = f32[2,16,4096]{2,1,0:T(8,128)S(1)} reshape(f32[2,8,2,2048,2]{4,3,2,1,0:T(8,128)} %broadcast_in_dim.20) | data formatting | bytes 1048576 | tf_op jit(solution)/shard_map/reshape | solution.py:119
  293.8 3.6 %collective-permute-done.47 = f32[2,1,4096]{2,1,0:T(1,128)S(1)} collective-permute-done((f32[2,1,4096]{2,1,0:T(1,128)S(1)}, f32[2,1,4096]{2,1,0:T(1,128)S(1)}, u32[]{:S(2)}, u32[]{:S(2)}) %collective-permute-start.47) | collective-permute-done | bytes 32800 | tf_op jit(solution)/shard_map/ppermute | solution.py:27
  302.5 3.6 %collective-permute-done.49 = f32[2,1,4096]{2,1,0:T(1,128)S(1)} collective-permute-done((f32[2,1,4096]{2,1,0:T(1,128)S(1)}, f32[2,1,4096]{2,1,0:T(1,128)S(1)}, u32[]{:S(2)}, u32[]{:S(2)}) %collective-permute-start.49) | collective-permute-done | bytes 32800 | tf_op jit(solution)/shard_map/ppermute | solution.py:27
  (199 shorter events, 87.6 us)
Async XLA Ops:
  1.8 16.0 %collective-permute-start.2 = (f32[2,1,4096]{2,1,0:T(1,128)S(1)}, f32[2,1,4096]{2,1,0:T(1,128)S(1)}, u32[]{:S(2)}, u32[]{:S(2)}) collective-permute-start(f32[2,1,4096]{2,1,0:T(1,128)S(1)} %get-tuple-element.68), channel_id=1, source_target_pairs={{1,0},{2,1},{3,2},{4,3},{5,4},{6,5},{7,6},{8,7},{9,8},{10,9},{11,1... | collective-permute-start | bytes 98312 | tf_op jit(solution)/shard_map/ppermute | solution.py:29
  4.5 13.2 %collective-permute-start.3 = (f32[2,1,4096]{2,1,0:T(1,128)S(1)}, f32[2,1,4096]{2,1,0:T(1,128)S(1)}, u32[]{:S(2)}, u32[]{:S(2)}) collective-permute-start(f32[2,1,4096]{2,1,0:T(1,128)S(1)} %get-tuple-element.69), channel_id=1, source_target_pairs={{0,1},{1,2},{2,3},{3,4},{4,5},{5,6},{6,7},{7,8},{8,9},{9,10},{10,1... | collective-permute-start | bytes 98312 | tf_op jit(solution)/shard_map/ppermute | solution.py:27
  7.8 6.8 %collective-permute-start = (f32[2,2,1,4096]{3,2,1,0:T(1,128)S(1)}, f32[2,2,1,4096]{3,2,1,0:T(1,128)S(1)}, u32[]{:S(2)}, u32[]{:S(2)}) collective-permute-start(f32[2,2,1,4096]{3,2,1,0:T(1,128)S(1)} %get-tuple-element.14), channel_id=1, source_target_pairs={{0,1},{1,2},{2,3},{3,4},{4,5},{5,6},{6,7},{7,8},{8,9},{9,10},{10,1... | collective-permute-start | bytes 196616 | tf_op jit(solution)/shard_map/ppermute | solution.py:27
  10.5 5.7 %collective-permute-start.1 = (f32[2,2,1,4096]{3,2,1,0:T(1,128)S(1)}, f32[2,2,1,4096]{3,2,1,0:T(1,128)S(1)}, u32[]{:S(2)}, u32[]{:S(2)}) collective-permute-start(f32[2,2,1,4096]{3,2,1,0:T(1,128)S(1)} %get-tuple-element.15), channel_id=1, source_target_pairs={{1,0},{2,1},{3,2},{4,3},{5,4},{6,5},{7,6},{8,7},{9,8},{10,9},{11,1... | collective-permute-start | bytes 196616 | tf_op jit(solution)/shard_map/ppermute | solution.py:29
  20.0 6.6 %collective-permute-start.4 = (f32[2,1,4096]{2,1,0:T(1,128)S(1)}, f32[2,1,4096]{2,1,0:T(1,128)S(1)}, u32[]{:S(2)}, u32[]{:S(2)}) collective-permute-start(f32[2,1,4096]{2,1,0:T(1,128)S(1)} %get-tuple-element.62), channel_id=1, source_target_pairs={{1,0},{2,1},{3,2},{4,3},{5,4},{6,5},{7,6},{8,7},{9,8},{10,9},{11,1... | collective-permute-start | bytes 98312 | tf_op jit(solution)/shard_map/ppermute | solution.py:29
  24.6 6.1 %collective-permute-start.5 = (f32[2,1,4096]{2,1,0:T(1,128)S(1)}, f32[2,1,4096]{2,1,0:T(1,128)S(1)}, u32[]{:S(2)}, u32[]{:S(2)}) collective-permute-start(f32[2,1,4096]{2,1,0:T(1,128)S(1)} %get-tuple-element.63), channel_id=1, source_target_pairs={{0,1},{1,2},{2,3},{3,4},{4,5},{5,6},{6,7},{7,8},{8,9},{9,10},{10,1... | collective-permute-start | bytes 98312 | tf_op jit(solution)/shard_map/ppermute | solution.py:27
  31.4 4.9 %collective-permute-start.6 = (f32[2,1,4096]{2,1,0:T(1,128)S(1)}, f32[2,1,4096]{2,1,0:T(1,128)S(1)}, u32[]{:S(2)}, u32[]{:S(2)}) collective-permute-start(f32[2,1,4096]{2,1,0:T(1,128)S(1)} %get-tuple-element.56), channel_id=1, source_target_pairs={{1,0},{2,1},{3,2},{4,3},{5,4},{6,5},{7,6},{8,7},{9,8},{10,9},{11,1... | collective-permute-start | bytes 98312 | tf_op jit(solution)/shard_map/ppermute | solution.py:29
  33.3 6.1 %collective-permute-start.7 = (f32[2,1,4096]{2,1,0:T(1,128)S(1)}, f32[2,1,4096]{2,1,0:T(1,128)S(1)}, u32[]{:S(2)}, u32[]{:S(2)}) collective-permute-start(f32[2,1,4096]{2,1,0:T(1,128)S(1)} %get-tuple-element.57), channel_id=1, source_target_pairs={{0,1},{1,2},{2,3},{3,4},{4,5},{5,6},{6,7},{7,8},{8,9},{9,10},{10,1... | collective-permute-start | bytes 98312 | tf_op jit(solution)/shard_map/ppermute | solution.py:27
  57.9 4.4 %collective-permute-start.8 = (f32[2,1,2048]{2,1,0:T(1,128)S(1)}, f32[2,1,2048]{2,1,0:T(1,128)S(1)}, u32[]{:S(2)}, u32[]{:S(2)}) collective-permute-start(f32[2,1,2048]{2,1,0:T(1,128)S(1)} %get-tuple-element.92), channel_id=1, source_target_pairs={{1,0},{2,1},{3,2},{4,3},{5,4},{6,5},{7,6},{8,7},{9,8},{10,9},{11,1... | collective-permute-start | bytes 49160 | tf_op jit(solution)/shard_map/ppermute | solution.py:29
  59.8 6.0 %collective-permute-start.9 = (f32[2,1,2048]{2,1,0:T(1,128)S(1)}, f32[2,1,2048]{2,1,0:T(1,128)S(1)}, u32[]{:S(2)}, u32[]{:S(2)}) collective-permute-start(f32[2,1,2048]{2,1,0:T(1,128)S(1)} %get-tuple-element.93), channel_id=1, source_target_pairs={{0,1},{1,2},{2,3},{3,4},{4,5},{5,6},{6,7},{7,8},{8,9},{9,10},{10,1... | collective-permute-start | bytes 49160 | tf_op jit(solution)/shard_map/ppermute | solution.py:27
  66.0 4.4 %collective-permute-start.10 = (f32[2,1,2048]{2,1,0:T(1,128)S(1)}, f32[2,1,2048]{2,1,0:T(1,128)S(1)}, u32[]{:S(2)}, u32[]{:S(2)}) collective-permute-start(f32[2,1,2048]{2,1,0:T(1,128)S(1)} %get-tuple-element.86), channel_id=1, source_target_pairs={{1,0},{2,1},{3,2},{4,3},{5,4},{6,5},{7,6},{8,7},{9,8},{10,9},{11,1... | collective-permute-start | bytes 49160 | tf_op jit(solution)/shard_map/ppermute | solution.py:29
  68.0 6.0 %collective-permute-start.11 = (f32[2,1,2048]{2,1,0:T(1,128)S(1)}, f32[2,1,2048]{2,1,0:T(1,128)S(1)}, u32[]{:S(2)}, u32[]{:S(2)}) collective-permute-start(f32[2,1,2048]{2,1,0:T(1,128)S(1)} %get-tuple-element.87), channel_id=1, source_target_pairs={{0,1},{1,2},{2,3},{3,4},{4,5},{5,6},{6,7},{7,8},{8,9},{9,10},{10,1... | collective-permute-start | bytes 49160 | tf_op jit(solution)/shard_map/ppermute | solution.py:27
  78.9 4.4 %collective-permute-start.12 = (f32[2,1,1024]{2,1,0:T(1,128)S(1)}, f32[2,1,1024]{2,1,0:T(1,128)S(1)}, u32[]{:S(2)}, u32[]{:S(2)}) collective-permute-start(f32[2,1,1024]{2,1,0:T(1,128)S(1)} %get-tuple-element.116), channel_id=1, source_target_pairs={{1,0},{2,1},{3,2},{4,3},{5,4},{6,5},{7,6},{8,7},{9,8},{10,9},{11,1... | collective-permute-start | bytes 24584 | tf_op jit(solution)/shard_map/ppermute | solution.py:29
  80.8 5.9 %collective-permute-start.13 = (f32[2,1,1024]{2,1,0:T(1,128)S(1)}, f32[2,1,1024]{2,1,0:T(1,128)S(1)}, u32[]{:S(2)}, u32[]{:S(2)}) collective-permute-start(f32[2,1,1024]{2,1,0:T(1,128)S(1)} %get-tuple-element.117), channel_id=1, source_target_pairs={{0,1},{1,2},{2,3},{3,4},{4,5},{5,6},{6,7},{7,8},{8,9},{9,10},{10,1... | collective-permute-start | bytes 24584 | tf_op jit(solution)/shard_map/ppermute | solution.py:27
  86.9 4.6 %collective-permute-start.14 = (f32[2,1,1024]{2,1,0:T(1,128)S(1)}, f32[2,1,1024]{2,1,0:T(1,128)S(1)}, u32[]{:S(2)}, u32[]{:S(2)}) collective-permute-start(f32[2,1,1024]{2,1,0:T(1,128)S(1)} %get-tuple-element.110), channel_id=1, source_target_pairs={{1,0},{2,1},{3,2},{4,3},{5,4},{6,5},{7,6},{8,7},{9,8},{10,9},{11,1... | collective-permute-start | bytes 24584 | tf_op jit(solution)/shard_map/ppermute | solution.py:29
  88.8 5.9 %collective-permute-start.15 = (f32[2,1,1024]{2,1,0:T(1,128)S(1)}, f32[2,1,1024]{2,1,0:T(1,128)S(1)}, u32[]{:S(2)}, u32[]{:S(2)}) collective-permute-start(f32[2,1,1024]{2,1,0:T(1,128)S(1)} %get-tuple-element.111), channel_id=1, source_target_pairs={{0,1},{1,2},{2,3},{3,4},{4,5},{5,6},{6,7},{7,8},{8,9},{9,10},{10,1... | collective-permute-start | bytes 24584 | tf_op jit(solution)/shard_map/ppermute | solution.py:27
  96.4 4.4 %collective-permute-start.16 = (f32[2,1,512]{2,1,0:T(1,128)S(1)}, f32[2,1,512]{2,1,0:T(1,128)S(1)}, u32[]{:S(2)}, u32[]{:S(2)}) collective-permute-start(f32[2,1,512]{2,1,0:T(1,128)S(1)} %get-tuple-element.136), channel_id=1, source_target_pairs={{1,0},{2,1},{3,2},{4,3},{5,4},{6,5},{7,6},{8,7},{9,8},{10,9},{11,1... | collective-permute-start | bytes 12296 | tf_op jit(solution)/shard_map/ppermute | solution.py:29
  98.4 5.8 %collective-permute-start.17 = (f32[2,1,512]{2,1,0:T(1,128)S(1)}, f32[2,1,512]{2,1,0:T(1,128)S(1)}, u32[]{:S(2)}, u32[]{:S(2)}) collective-permute-start(f32[2,1,512]{2,1,0:T(1,128)S(1)} %get-tuple-element.137), channel_id=1, source_target_pairs={{0,1},{1,2},{2,3},{3,4},{4,5},{5,6},{6,7},{7,8},{8,9},{9,10},{10,1... | collective-permute-start | bytes 12296 | tf_op jit(solution)/shard_map/ppermute | solution.py:27
  106.3 5.8 %collective-permute-start.19 = (f32[2,1,512]{2,1,0:T(1,128)S(1)}, f32[2,1,512]{2,1,0:T(1,128)S(1)}, u32[]{:S(2)}, u32[]{:S(2)}) collective-permute-start(f32[2,1,512]{2,1,0:T(1,128)S(1)} %get-tuple-element.131), channel_id=1, source_target_pairs={{0,1},{1,2},{2,3},{3,4},{4,5},{5,6},{6,7},{7,8},{8,9},{9,10},{10,1... | collective-permute-start | bytes 12296 | tf_op jit(solution)/shard_map/ppermute | solution.py:27
  113.3 6.5 %collective-permute-start.21 = (f32[2,1,256]{2,1,0:T(1,128)S(1)}, f32[2,1,256]{2,1,0:T(1,128)S(1)}, u32[]{:S(2)}, u32[]{:S(2)}) collective-permute-start(f32[2,1,256]{2,1,0:T(1,128)S(1)} %get-tuple-element.2), channel_id=1, source_target_pairs={{0,1},{1,2},{2,3},{3,4},{4,5},{5,6},{6,7},{7,8},{8,9},{9,10},{10,1... | collective-permute-start | bytes 6152 | tf_op jit(solution)/shard_map/ppermute | solution.py:27
  115.2 5.8 %collective-permute-start.20 = (f32[2,1,256]{2,1,0:T(1,128)S(1)}, f32[2,1,256]{2,1,0:T(1,128)S(1)}, u32[]{:S(2)}, u32[]{:S(2)}) collective-permute-start(f32[2,1,256]{2,1,0:T(1,128)S(1)} %get-tuple-element.2), channel_id=1, source_target_pairs={{1,0},{2,1},{3,2},{4,3},{5,4},{6,5},{7,6},{8,7},{9,8},{10,9},{11,1... | collective-permute-start | bytes 6152 | tf_op jit(solution)/shard_map/ppermute | solution.py:29
  121.2 6.5 %collective-permute-start.23 = (f32[2,1,256]{2,1,0:T(1,128)S(1)}, f32[2,1,256]{2,1,0:T(1,128)S(1)}, u32[]{:S(2)}, u32[]{:S(2)}) collective-permute-start(f32[2,1,256]{2,1,0:T(1,128)S(1)} %multiply_add_fusion.9), channel_id=1, source_target_pairs={{0,1},{1,2},{2,3},{3,4},{4,5},{5,6},{6,7},{7,8},{8,9},{9,10},{10,1... | collective-permute-start | bytes 6152 | tf_op jit(solution)/shard_map/ppermute | solution.py:27
  123.1 5.8 %collective-permute-start.22 = (f32[2,1,256]{2,1,0:T(1,128)S(1)}, f32[2,1,256]{2,1,0:T(1,128)S(1)}, u32[]{:S(2)}, u32[]{:S(2)}) collective-permute-start(f32[2,1,256]{2,1,0:T(1,128)S(1)} %multiply_add_fusion.9), channel_id=1, source_target_pairs={{1,0},{2,1},{3,2},{4,3},{5,4},{6,5},{7,6},{8,7},{9,8},{10,9},{11,1... | collective-permute-start | bytes 6152 | tf_op jit(solution)/shard_map/ppermute | solution.py:29
  129.1 6.5 %collective-permute-start.25 = (f32[2,1,256]{2,1,0:T(1,128)S(1)}, f32[2,1,256]{2,1,0:T(1,128)S(1)}, u32[]{:S(2)}, u32[]{:S(2)}) collective-permute-start(f32[2,1,256]{2,1,0:T(1,128)S(1)} %multiply_add_fusion.8), channel_id=1, source_target_pairs={{0,1},{1,2},{2,3},{3,4},{4,5},{5,6},{6,7},{7,8},{8,9},{9,10},{10,1... | collective-permute-start | bytes 6152 | tf_op jit(solution)/shard_map/ppermute | solution.py:27
  131.6 5.3 %collective-permute-start.24 = (f32[2,1,256]{2,1,0:T(1,128)S(1)}, f32[2,1,256]{2,1,0:T(1,128)S(1)}, u32[]{:S(2)}, u32[]{:S(2)}) collective-permute-start(f32[2,1,256]{2,1,0:T(1,128)S(1)} %multiply_add_fusion.8), channel_id=1, source_target_pairs={{1,0},{2,1},{3,2},{4,3},{5,4},{6,5},{7,6},{8,7},{9,8},{10,9},{11,1... | collective-permute-start | bytes 6152 | tf_op jit(solution)/shard_map/ppermute | solution.py:29
  137.0 6.5 %collective-permute-start.27 = (f32[2,1,256]{2,1,0:T(1,128)S(1)}, f32[2,1,256]{2,1,0:T(1,128)S(1)}, u32[]{:S(2)}, u32[]{:S(2)}) collective-permute-start(f32[2,1,256]{2,1,0:T(1,128)S(1)} %multiply_add_fusion.7), channel_id=1, source_target_pairs={{0,1},{1,2},{2,3},{3,4},{4,5},{5,6},{6,7},{7,8},{8,9},{9,10},{10,1... | collective-permute-start | bytes 6152 | tf_op jit(solution)/shard_map/ppermute | solution.py:27
  139.5 5.3 %collective-permute-start.26 = (f32[2,1,256]{2,1,0:T(1,128)S(1)}, f32[2,1,256]{2,1,0:T(1,128)S(1)}, u32[]{:S(2)}, u32[]{:S(2)}) collective-permute-start(f32[2,1,256]{2,1,0:T(1,128)S(1)} %multiply_add_fusion.7), channel_id=1, source_target_pairs={{1,0},{2,1},{3,2},{4,3},{5,4},{6,5},{7,6},{8,7},{9,8},{10,9},{11,1... | collective-permute-start | bytes 6152 | tf_op jit(solution)/shard_map/ppermute | solution.py:29
  144.9 6.5 %collective-permute-start.29 = (f32[2,1,256]{2,1,0:T(1,128)S(1)}, f32[2,1,256]{2,1,0:T(1,128)S(1)}, u32[]{:S(2)}, u32[]{:S(2)}) collective-permute-start(f32[2,1,256]{2,1,0:T(1,128)S(1)} %multiply_add_fusion.6), channel_id=1, source_target_pairs={{0,1},{1,2},{2,3},{3,4},{4,5},{5,6},{6,7},{7,8},{8,9},{9,10},{10,1... | collective-permute-start | bytes 6152 | tf_op jit(solution)/shard_map/ppermute | solution.py:27
  147.4 5.3 %collective-permute-start.28 = (f32[2,1,256]{2,1,0:T(1,128)S(1)}, f32[2,1,256]{2,1,0:T(1,128)S(1)}, u32[]{:S(2)}, u32[]{:S(2)}) collective-permute-start(f32[2,1,256]{2,1,0:T(1,128)S(1)} %multiply_add_fusion.6), channel_id=1, source_target_pairs={{1,0},{2,1},{3,2},{4,3},{5,4},{6,5},{7,6},{8,7},{9,8},{10,9},{11,1... | collective-permute-start | bytes 6152 | tf_op jit(solution)/shard_map/ppermute | solution.py:29
  152.9 6.5 %collective-permute-start.31 = (f32[2,1,256]{2,1,0:T(1,128)S(1)}, f32[2,1,256]{2,1,0:T(1,128)S(1)}, u32[]{:S(2)}, u32[]{:S(2)}) collective-permute-start(f32[2,1,256]{2,1,0:T(1,128)S(1)} %multiply_add_fusion.5), channel_id=1, source_target_pairs={{0,1},{1,2},{2,3},{3,4},{4,5},{5,6},{6,7},{7,8},{8,9},{9,10},{10,1... | collective-permute-start | bytes 6152 | tf_op jit(solution)/shard_map/ppermute | solution.py:27
  155.3 5.3 %collective-permute-start.30 = (f32[2,1,256]{2,1,0:T(1,128)S(1)}, f32[2,1,256]{2,1,0:T(1,128)S(1)}, u32[]{:S(2)}, u32[]{:S(2)}) collective-permute-start(f32[2,1,256]{2,1,0:T(1,128)S(1)} %multiply_add_fusion.5), channel_id=1, source_target_pairs={{1,0},{2,1},{3,2},{4,3},{5,4},{6,5},{7,6},{8,7},{9,8},{10,9},{11,1... | collective-permute-start | bytes 6152 | tf_op jit(solution)/shard_map/ppermute | solution.py:29
  160.8 6.5 %collective-permute-start.33 = (f32[2,1,256]{2,1,0:T(1,128)S(1)}, f32[2,1,256]{2,1,0:T(1,128)S(1)}, u32[]{:S(2)}, u32[]{:S(2)}) collective-permute-start(f32[2,1,256]{2,1,0:T(1,128)S(1)} %multiply_add_fusion.4), channel_id=1, source_target_pairs={{0,1},{1,2},{2,3},{3,4},{4,5},{5,6},{6,7},{7,8},{8,9},{9,10},{10,1... | collective-permute-start | bytes 6152 | tf_op jit(solution)/shard_map/ppermute | solution.py:27
  163.2 5.3 %collective-permute-start.32 = (f32[2,1,256]{2,1,0:T(1,128)S(1)}, f32[2,1,256]{2,1,0:T(1,128)S(1)}, u32[]{:S(2)}, u32[]{:S(2)}) collective-permute-start(f32[2,1,256]{2,1,0:T(1,128)S(1)} %multiply_add_fusion.4), channel_id=1, source_target_pairs={{1,0},{2,1},{3,2},{4,3},{5,4},{6,5},{7,6},{8,7},{9,8},{10,9},{11,1... | collective-permute-start | bytes 6152 | tf_op jit(solution)/shard_map/ppermute | solution.py:29
  169.1 6.5 %collective-permute-start.34 = (f32[2,1,512]{2,1,0:T(1,128)S(1)}, f32[2,1,512]{2,1,0:T(1,128)S(1)}, u32[]{:S(2)}, u32[]{:S(2)}) collective-permute-start(f32[2,1,512]{2,1,0:T(1,128)S(1)} %get-tuple-element.124), channel_id=1, source_target_pairs={{1,0},{2,1},{3,2},{4,3},{5,4},{6,5},{7,6},{8,7},{9,8},{10,9},{11,1... | collective-permute-start | bytes 12296 | tf_op jit(solution)/shard_map/ppermute | solution.py:29
  173.6 5.8 %collective-permute-start.35 = (f32[2,1,512]{2,1,0:T(1,128)S(1)}, f32[2,1,512]{2,1,0:T(1,128)S(1)}, u32[]{:S(2)}, u32[]{:S(2)}) collective-permute-start(f32[2,1,512]{2,1,0:T(1,128)S(1)} %get-tuple-element.125), channel_id=1, source_target_pairs={{0,1},{1,2},{2,3},{3,4},{4,5},{5,6},{6,7},{7,8},{8,9},{9,10},{10,1... | collective-permute-start | bytes 12296 | tf_op jit(solution)/shard_map/ppermute | solution.py:27
  181.5 5.8 %collective-permute-start.37 = (f32[2,1,512]{2,1,0:T(1,128)S(1)}, f32[2,1,512]{2,1,0:T(1,128)S(1)}, u32[]{:S(2)}, u32[]{:S(2)}) collective-permute-start(f32[2,1,512]{2,1,0:T(1,128)S(1)} %get-tuple-element.119), channel_id=1, source_target_pairs={{0,1},{1,2},{2,3},{3,4},{4,5},{5,6},{6,7},{7,8},{8,9},{9,10},{10,1... | collective-permute-start | bytes 12296 | tf_op jit(solution)/shard_map/ppermute | solution.py:27
  189.1 4.4 %collective-permute-start.38 = (f32[2,1,1024]{2,1,0:T(1,128)S(1)}, f32[2,1,1024]{2,1,0:T(1,128)S(1)}, u32[]{:S(2)}, u32[]{:S(2)}) collective-permute-start(f32[2,1,1024]{2,1,0:T(1,128)S(1)} %get-tuple-element.104), channel_id=1, source_target_pairs={{1,0},{2,1},{3,2},{4,3},{5,4},{6,5},{7,6},{8,7},{9,8},{10,9},{11,1... | collective-permute-start | bytes 24584 | tf_op jit(solution)/shard_map/ppermute | solution.py:29
  191.0 5.9 %collective-permute-start.39 = (f32[2,1,1024]{2,1,0:T(1,128)S(1)}, f32[2,1,1024]{2,1,0:T(1,128)S(1)}, u32[]{:S(2)}, u32[]{:S(2)}) collective-permute-start(f32[2,1,1024]{2,1,0:T(1,128)S(1)} %get-tuple-element.105), channel_id=1, source_target_pairs={{0,1},{1,2},{2,3},{3,4},{4,5},{5,6},{6,7},{7,8},{8,9},{9,10},{10,1... | collective-permute-start | bytes 24584 | tf_op jit(solution)/shard_map/ppermute | solution.py:27
  197.1 4.4 %collective-permute-start.40 = (f32[2,1,1024]{2,1,0:T(1,128)S(1)}, f32[2,1,1024]{2,1,0:T(1,128)S(1)}, u32[]{:S(2)}, u32[]{:S(2)}) collective-permute-start(f32[2,1,1024]{2,1,0:T(1,128)S(1)} %get-tuple-element.98), channel_id=1, source_target_pairs={{1,0},{2,1},{3,2},{4,3},{5,4},{6,5},{7,6},{8,7},{9,8},{10,9},{11,1... | collective-permute-start | bytes 24584 | tf_op jit(solution)/shard_map/ppermute | solution.py:29
  199.0 5.9 %collective-permute-start.41 = (f32[2,1,1024]{2,1,0:T(1,128)S(1)}, f32[2,1,1024]{2,1,0:T(1,128)S(1)}, u32[]{:S(2)}, u32[]{:S(2)}) collective-permute-start(f32[2,1,1024]{2,1,0:T(1,128)S(1)} %get-tuple-element.99), channel_id=1, source_target_pairs={{0,1},{1,2},{2,3},{3,4},{4,5},{5,6},{6,7},{7,8},{8,9},{9,10},{10,1... | collective-permute-start | bytes 24584 | tf_op jit(solution)/shard_map/ppermute | solution.py:27
  217.9 4.4 %collective-permute-start.42 = (f32[2,1,2048]{2,1,0:T(1,128)S(1)}, f32[2,1,2048]{2,1,0:T(1,128)S(1)}, u32[]{:S(2)}, u32[]{:S(2)}) collective-permute-start(f32[2,1,2048]{2,1,0:T(1,128)S(1)} %get-tuple-element.80), channel_id=1, source_target_pairs={{1,0},{2,1},{3,2},{4,3},{5,4},{6,5},{7,6},{8,7},{9,8},{10,9},{11,1... | collective-permute-start | bytes 49160 | tf_op jit(solution)/shard_map/ppermute | solution.py:29
  219.8 6.0 %collective-permute-start.43 = (f32[2,1,2048]{2,1,0:T(1,128)S(1)}, f32[2,1,2048]{2,1,0:T(1,128)S(1)}, u32[]{:S(2)}, u32[]{:S(2)}) collective-permute-start(f32[2,1,2048]{2,1,0:T(1,128)S(1)} %get-tuple-element.81), channel_id=1, source_target_pairs={{0,1},{1,2},{2,3},{3,4},{4,5},{5,6},{6,7},{7,8},{8,9},{9,10},{10,1... | collective-permute-start | bytes 49160 | tf_op jit(solution)/shard_map/ppermute | solution.py:27
  226.0 4.7 %collective-permute-start.44 = (f32[2,1,2048]{2,1,0:T(1,128)S(1)}, f32[2,1,2048]{2,1,0:T(1,128)S(1)}, u32[]{:S(2)}, u32[]{:S(2)}) collective-permute-start(f32[2,1,2048]{2,1,0:T(1,128)S(1)} %get-tuple-element.74), channel_id=1, source_target_pairs={{1,0},{2,1},{3,2},{4,3},{5,4},{6,5},{7,6},{8,7},{9,8},{10,9},{11,1... | collective-permute-start | bytes 49160 | tf_op jit(solution)/shard_map/ppermute | solution.py:29
  228.0 6.0 %collective-permute-start.45 = (f32[2,1,2048]{2,1,0:T(1,128)S(1)}, f32[2,1,2048]{2,1,0:T(1,128)S(1)}, u32[]{:S(2)}, u32[]{:S(2)}) collective-permute-start(f32[2,1,2048]{2,1,0:T(1,128)S(1)} %get-tuple-element.75), channel_id=1, source_target_pairs={{0,1},{1,2},{2,3},{3,4},{4,5},{5,6},{6,7},{7,8},{8,9},{9,10},{10,1... | collective-permute-start | bytes 49160 | tf_op jit(solution)/shard_map/ppermute | solution.py:27
  289.4 4.4 %collective-permute-start.46 = (f32[2,1,4096]{2,1,0:T(1,128)S(1)}, f32[2,1,4096]{2,1,0:T(1,128)S(1)}, u32[]{:S(2)}, u32[]{:S(2)}) collective-permute-start(f32[2,1,4096]{2,1,0:T(1,128)S(1)} %get-tuple-element.50), channel_id=1, source_target_pairs={{1,0},{2,1},{3,2},{4,3},{5,4},{6,5},{7,6},{8,7},{9,8},{10,9},{11,1... | collective-permute-start | bytes 98312 | tf_op jit(solution)/shard_map/ppermute | solution.py:29
  291.3 6.1 %collective-permute-start.47 = (f32[2,1,4096]{2,1,0:T(1,128)S(1)}, f32[2,1,4096]{2,1,0:T(1,128)S(1)}, u32[]{:S(2)}, u32[]{:S(2)}) collective-permute-start(f32[2,1,4096]{2,1,0:T(1,128)S(1)} %get-tuple-element.51), channel_id=1, source_target_pairs={{0,1},{1,2},{2,3},{3,4},{4,5},{5,6},{6,7},{7,8},{8,9},{9,10},{10,1... | collective-permute-start | bytes 98312 | tf_op jit(solution)/shard_map/ppermute | solution.py:27
  298.1 4.4 %collective-permute-start.48 = (f32[2,1,4096]{2,1,0:T(1,128)S(1)}, f32[2,1,4096]{2,1,0:T(1,128)S(1)}, u32[]{:S(2)}, u32[]{:S(2)}) collective-permute-start(f32[2,1,4096]{2,1,0:T(1,128)S(1)} %get-tuple-element.44), channel_id=1, source_target_pairs={{1,0},{2,1},{3,2},{4,3},{5,4},{6,5},{7,6},{8,7},{9,8},{10,9},{11,1... | collective-permute-start | bytes 98312 | tf_op jit(solution)/shard_map/ppermute | solution.py:29
  300.0 6.1 %collective-permute-start.49 = (f32[2,1,4096]{2,1,0:T(1,128)S(1)}, f32[2,1,4096]{2,1,0:T(1,128)S(1)}, u32[]{:S(2)}, u32[]{:S(2)}) collective-permute-start(f32[2,1,4096]{2,1,0:T(1,128)S(1)} %get-tuple-element.45), channel_id=1, source_target_pairs={{0,1},{1,2},{2,3},{3,4},{4,5},{5,6},{6,7},{7,8},{8,9},{9,10},{10,1... | collective-permute-start | bytes 98312 | tf_op jit(solution)/shard_map/ppermute | solution.py:27
  (12 other events, 439.3 us)
where the time goes:
time: 313 us; the launch traced here: 308 us
  starting transfers between devices  131 us (42%)
  local copies, waits for them, and re-layouts  101 us (32%)
  waiting for transfers between devices  65.5 us (21%)
  other arithmetic  8.23 us (3%)
    ppermute x25, starting transfers between devices, extended(): lax.ppermute(head, axis, [((i + 1) % count, i) for i in range(ends)])  71.6 us
    ppermute x25, starting transfers between devices, extended(): lax.ppermute(tail, axis, [(i, (i + 1) % count) for i in range(ends)])  59.1 us
    ppermute x25, waiting for transfers between devices, extended(): lax.ppermute(tail, axis, [(i, (i + 1) % count) for i in range(ends)])  55.3 us
    reshape x3, local copies, waits for them, and re-layouts, prolong(): return spread.reshape(layers, 2 * row_count, 2 * col_count)  53.6 us
    broadcast_in_dim x5, local copies, waits for them, and re-layouts, prolong(): jnp.broadcast_to(correction[:, :, None, :, None], (layers, row_count, 2,...  16 us
    ppermute x25, waiting for transfers between devices, extended(): lax.ppermute(head, axis, [((i + 1) % count, i) for i in range(ends)])  10.1 us
    slice x4, local copies, waits for them, and re-layouts, restrict(): residual[:, 1::2, 0::2]  6.32 us
  transfers between devices with their start and end apart: 50, of which 24 were waited for; matrix products, arithmetic and copies ran while one was open for 2% of the time, Pallas kernels for 0%

commit v1 on v0

v1 whole, which is shorter than its diff:
```python
import functools

import jax
import jax.numpy as jnp
from jax import lax
from jax.experimental import pallas as pl
from jax.experimental.pallas import tpu as pltpu
from jax.sharding import PartitionSpec as P

MESH = pl.DeviceIdType.MESH
WEIGHT = 0.8
F = (0.02, 0.04)
DT = 0.5
BETA = 0.05
DRAG = 0.02

ROWS = 16
WIDTH = (4, 2, 1, 1, 1)
STEP = (1, 1, 1, 2, 4)
HALO = (4, 4, 5, 20, 9)
OWN = (16, 8, 4, 2, 1)
EXT = tuple(o + 2 * h for o, h in zip(OWN, HALO))
REACH = 10


def rows_loop(lo, hi, body, unroll=4):
    count = hi - lo
    if count <= unroll:
        for r in range(lo, hi):
            body(r)
        return
    trips = count // unroll

    def trip(i, carry):
        for j in range(unroll):
            body(lo + i * unroll + j)
        return carry

    lax.fori_loop(0, trips, trip, 0)
    for r in range(lo + trips * unroll, hi):
        body(r)


def kernel(n, pq_ref, qn_ref, sn_ref, pq, b0, a0, c0, b1, a1, c1, b2, a2, c2, b3, a3, c3, b4, a4, c4, send, recv):
    me = lax.axis_index("wide")
    sub = lax.broadcasted_iota(jnp.int32, (8, 128), 0)
    first = [sub < s for s in (1, 1, 1, 2, 4)]
    last = [sub >= 8 - s for s in (1, 1, 1, 2, 4)]
    odd1 = (sub & 1) != 0
    odd2 = (sub & 2) != 0
    zero = jnp.zeros((8, 128), jnp.float32)

    def east(v, level):
        s = STEP[level]
        z = pltpu.roll(v[0], 8 - s, 0)
        return v[1:] + [jnp.where(last[level], pltpu.roll(z, 127, 1), z)]

    def west(v, level):
        s = STEP[level]
        z = pltpu.roll(v[-1], s, 0)
        return [jnp.where(first[level], pltpu.roll(z, 1, 1), z)] + v[:-1]

    def mask(r, level):
        g = me * OWN[level] + r - HALO[level]
        return jnp.where(jnp.logical_and(g >= 0, g < n * OWN[level]), 1.0, 0.0).astype(jnp.float32)

    def load(ref, r, level):
        return [[ref[r, k, u] for u in range(WIDTH[level])] for k in range(2)]

    def load_p(ref, r, level):
        return [[ref[r, 0, k, u] for u in range(4)] for k in range(2)]

    def around(src, r, level, get):
        up, mid, down = get(src, r + 1, level), get(src, r, level), get(src, r - 1, level)
        nb = []
        for k in range(2):
            e, w = east(mid[k], level), west(mid[k], level)
            nb.append([up[k][u] + down[k][u] + (e[u] + w[u]) for u in range(WIDTH[level])])
        return mid, nb

    def sweep(src, dst, b, lo, hi, level, get=load, out=None, unroll=4):
        h2 = 4.0**level

        def body(r):
            m = mask(r, level)
            mid, nb = around(src, r, level, get)
            for k in range(2):
                c = m * (WEIGHT / (4.0 / h2 + F[k]))
                keep = m * (1.0 - WEIGHT)
                for u in range(WIDTH[level]):
                    new = keep * mid[k][u] + c * (
                        b[r, k, u] + nb[k][u] * (1.0 / h2) + F[k] * mid[1 - k][u]
                    )
                    if out is None:
                        dst[r, k, u] = new
                    else:
                        dst[r - HALO[level], k, u] = new

        rows_loop(lo, hi, body, unroll)

    def from_zero(dst, b, lo, hi, level):
        def body(r):
            m = mask(r, level)
            for k in range(2):
                c = m * (WEIGHT / (4.0 / 4.0**level + F[k]))
                for u in range(WIDTH[level]):
                    dst[r, k, u] = c * b[r, k, u]

        rows_loop(lo, hi, body)

    def residual(v, b, coarse, lo, count, at, level):
        h2 = 4.0**level
        wide = WIDTH[level]

        def body(i):
            total = [[zero] * wide for _ in range(2)]
            for j in range(2):
                r = lo + 2 * i + j
                mid, nb = around(v, r, level, load)
                for k in range(2):
                    for u in range(wide):
                        x = (
                            b[r, k, u]
                            + (nb[k][u] - 4.0 * mid[k][u]) * (1.0 / h2)
                            - F[k] * (mid[k][u] - mid[1 - k][u])
                        )
                        total[k][u] = x if j == 0 else total[k][u] + x
            for k in range(2):
                t = total[k]
                if level < 2:
                    for u in range(wide // 2):
                        coarse[at + i, k, u] = 0.25 * (t[2 * u] + t[2 * u + 1])
                else:
                    s = 1 if level == 2 else 2
                    odd = odd1 if level == 2 else odd2
                    other = jnp.where(odd, pltpu.roll(t[0], s, 0), pltpu.roll(t[0], 8 - s, 0))
                    coarse[at + i, k, 0] = 0.25 * (t[0] + other)

        rows_loop(0, count, body, 2)

    def prolong(v, coarse, lo, hi, level, shift):
        def body(r):
            i = (r + shift) // 2 if isinstance(r, int) else lax.div(r + shift, 2)
            for k in range(2):
                for u in range(WIDTH[level]):
                    cu = u // 2 if level < 2 else u
                    v[r, k, u] = v[r, k, u] + coarse[i, k, cu]

        rows_loop(lo, hi, body)

    def inside(d):
        return jnp.logical_and(me + d >= 0, me + d < n)

    copies = []

    def put(d, src, dst):
        copies.append((d, src, dst))
        return len(copies) - 1

    def copy(i, d, src, dst):
        return pltpu.make_async_remote_copy(
            src_ref=src,
            dst_ref=dst,
            send_sem=send.at[i],
            recv_sem=recv.at[i],
            device_id={"wide": me + d},
            device_id_type=MESH,
        )

    def start(ids):
        for i in ids:
            d, src, dst = copies[i]

            @pl.when(inside(d))
            def _():
                copy(i, d, src, dst).start()

    def arrive(ids):
        for i in ids:
            d, src, dst = copies[i]

            @pl.when(inside(-d))
            def _():
                copy(i, -d, src, dst).wait_recv()

    def depart(ids):
        for i in ids:
            d, src, dst = copies[i]

            @pl.when(inside(d))
            def _():
                copy(i, d, src, dst).wait_send()

    reach = min(REACH, n - 1)
    phase_a = [
        put(1, pq_ref.at[pl.ds(12, 4)], pq.at[pl.ds(0, 4)]),
        put(-1, pq_ref.at[pl.ds(0, 4)], pq.at[pl.ds(20, 4)]),
    ]
    phase_b = [
        put(1, b1.at[pl.ds(8, 4)], b1.at[pl.ds(0, 4)]),
        put(-1, b1.at[pl.ds(4, 4)], b1.at[pl.ds(12, 4)]),
    ]
    phase_c = [
        put(1, b2.at[pl.ds(5, 4)], b2.at[pl.ds(1, 4)]),
        put(-1, b2.at[pl.ds(5, 4)], b2.at[pl.ds(9, 4)]),
        put(2, b2.at[pl.ds(8, 1)], b2.at[pl.ds(0, 1)]),
        put(-2, b2.at[pl.ds(5, 1)], b2.at[pl.ds(13, 1)]),
    ]
    phase_d = []
    for d in range(reach, 0, -1):
        for signed in (d, -d):
            phase_d.append(put(signed, b3.at[pl.ds(20, 2)], b3.at[pl.ds(20 - 2 * signed, 2)]))

    def clear(ref, lo, hi, inner):
        for r in range(lo, hi):
            for index in inner:
                ref[(r, *index)] = zero

    pairs = [(k, u) for k in range(2) for u in range(4)]

    @pl.when(me == 0)
    def _():
        clear(pq, 0, 4, [(f, k, u) for f in range(2) for k, u in pairs])

    @pl.when(me == n - 1)
    def _():
        clear(pq, 20, 24, [(f, k, u) for f in range(2) for k, u in pairs])

    clear(b1, 0, 4, [(k, u) for k in range(2) for u in range(2)])
    clear(b1, 12, 16, [(k, u) for k in range(2) for u in range(2)])
    clear(b2, 0, 5, [(0, 0), (1, 0)])
    clear(b2, 9, 14, [(0, 0), (1, 0)])
    clear(b3, 0, 20, [(0, 0), (1, 0)])
    clear(b3, 22, 42, [(0, 0), (1, 0)])

    barrier = pltpu.get_barrier_semaphore()
    for d in range(-reach, reach + 1):
        if d:

            @pl.when(inside(d))
            def _():
                pl.semaphore_signal(barrier, inc=1, device_id={"wide": me + d}, device_id_type=MESH)

    pl.semaphore_wait(barrier, jnp.minimum(me, reach) + jnp.minimum(n - 1 - me, reach))

    start(phase_a)

    def take(r):
        for f in range(2):
            for k, u in pairs:
                pq[r + 4, f, k, u] = pq_ref[r, f, k, u]

    rows_loop(0, 16, take, 2)

    def advance(lo, hi, own):
        def body(r):
            for k in range(2):
                p = [[pq[r + j, 0, k, u] for u in range(4)] for j in (-1, 0, 1)]
                q = [[pq[r + j, 1, k, u] for u in range(4)] for j in (-1, 0, 1)]
                pe, pw = [east(x, 0) for x in p], [west(x, 0) for x in p]
                qe, qw = [east(x, 0) for x in q], [west(x, 0) for x in q]
                for u in range(4):
                    ps, pc, pn = (x[u] for x in p)
                    qs, qc, qnn = (x[u] for x in q)
                    pse, pce, pne = (x[u] for x in pe)
                    psw, pcw, pnw = (x[u] for x in pw)
                    qse, qce, qne = (x[u] for x in qe)
                    qsw, qcw, qnw = (x[u] for x in qw)
                    ns = qnn - qs
                    ew = qce - qcw
                    jac = (
                        pce * (ns + (qne - qse))
                        - pcw * (ns + (qnw - qsw))
                        - pn * (ew + (qne - qnw))
                        + ps * (ew + (qse - qsw))
                        + pne * (qnn - qce)
                        - pnw * (qnn - qcw)
                        - pse * (qs - qce)
                        + psw * (qs - qcw)
                    )
                    change = jac * (DT / 12.0) + (pce - pcw) * (DT * BETA * 0.5)
                    if k == 1:
                        change = change + (DT * DRAG) * ((pn + ps) + (pcw + pce) - 4.0 * pc)
                    b0[r, k, u] = change - qc
                    if own:
                        qn_ref[r - 4, k, u] = qc - change

        rows_loop(lo, hi, body, 1)

    advance(5, 19, True)
    arrive(phase_a)
    advance(1, 4, False)
    advance(4, 5, True)
    advance(19, 20, True)
    advance(20, 23, False)

    sweep(pq, a0, b0, 1, 23, 0, load_p, unroll=2)
    sweep(a0, c0, b0, 2, 22, 0, unroll=2)
    residual(c0, b0, b1, 4, 8, 4, 0)

    start(phase_b)
    arrive(phase_b)
    from_zero(a1, b1, 0, 16, 1)
    sweep(a1, c1, b1, 1, 15, 1)
    residual(c1, b1, b2, 4, 4, 5, 1)

    start(phase_c)
    arrive(phase_c)
    from_zero(a2, b2, 0, 14, 2)
    sweep(a2, c2, b2, 1, 13, 2)
    residual(c2, b2, b3, 5, 2, 20, 2)

    start(phase_d)
    arrive(phase_d)
    from_zero(a3, b3, 0, 42, 3)
    sweep(a3, c3, b3, 1, 41, 3)
    residual(c3, b3, b4, 2, 19, 0, 3)

    from_zero(a4, b4, 0, 19, 4)
    x, y = a4, c4
    for j in range(1, 8):
        sweep(x, y, b4, j, 19 - j, 4)
        x, y = y, x

    prolong(c3, x, 16, 26, 3, -2)
    sweep(c3, a3, b3, 17, 25, 3)
    sweep(a3, c3, b3, 18, 24, 3)

    prolong(c2, c3, 1, 13, 2, 35)
    sweep(c2, a2, b2, 2, 12, 2)
    sweep(a2, c2, b2, 3, 11, 2)

    prolong(c1, c2, 1, 15, 1, 6)
    sweep(c1, a1, b1, 2, 14, 1)
    sweep(a1, c1, b1, 3, 13, 1)

    prolong(c0, c1, 2, 22, 0, 4)
    sweep(c0, a0, b0, 3, 21, 0, unroll=2)
    sweep(a0, sn_ref, b0, 4, 20, 0, out=True, unroll=2)

    depart(range(len(copies)))


def spread(x):
    layers, rows, cols = x.shape
    return x.reshape(layers, rows, 128, 8, 4).transpose(1, 0, 4, 3, 2)


def gather(x):
    rows, layers = x.shape[:2]
    return x.transpose(1, 0, 4, 3, 2).reshape(layers, rows, 4096)


def shards(stream_now, vorticity):
    n = lax.axis_size("wide")
    pq = jnp.stack([spread(stream_now), spread(vorticity)], axis=1)
    vmem = pl.BlockSpec(memory_space=pltpu.VMEM)
    shape = jax.ShapeDtypeStruct((ROWS, 2, 4, 8, 128), jnp.float32)
    scratch = [pltpu.VMEM((EXT[0], 2, 2, 4, 8, 128), jnp.float32)]
    for level in range(5):
        scratch += [pltpu.VMEM((EXT[level], 2, WIDTH[level], 8, 128), jnp.float32)] * 3
    count = 8 + 2 * min(REACH, n - 1)
    qn, sn = pl.pallas_call(
        functools.partial(kernel, n),
        out_shape=(shape, shape),
        in_specs=[vmem],
        out_specs=(vmem, vmem),
        scratch_shapes=scratch
        + [pltpu.SemaphoreType.DMA((count,)), pltpu.SemaphoreType.DMA((count,))],
        compiler_params=pltpu.CompilerParams(
            collective_id=0, has_side_effects=True, vmem_limit_bytes=40 * 1024 * 1024
        ),
    )(pq)
    return gather(qn), gather(sn)


def solution(mesh):
    return jax.shard_map(
        shards,
        mesh=mesh,
        in_specs=(P("member", "wide", None), P("member", "wide", None)),
        out_specs=(P("member", "wide", None), P("member", "wide", None)),
        check_vma=False,
    )
```

time: 313 us -> 65.3 us (0.21)
  the two profiles are of different devices: /device:TPU:8 before, /device:TPU:0 now
where the time goes in v1:
time: 65.3 us; the launch traced here: 65.2 us
  Pallas kernels  34.7 us (53%)
  local copies, waits for them, and re-layouts  29.7 us (45%)
  between operations  0.68 us (1%)
    pallas_call x1, Pallas kernels, shards(): pl.pallas_call(functools.partial(kernel, n), out_shape=(shape, shape), in...  34.7 us
    unnamed x6, local copies, waits for them, and re-layouts  13.2 us
    transpose x2, local copies, waits for them, and re-layouts, gather(): return x.transpose(1, 0, 4, 3, 2).reshape(layers, rows, 4096)  8.71 us
    reshape x2, local copies, waits for them, and re-layouts, spread(): return x.reshape(layers, rows, 128, 8, 4).transpose(1, 0, 4, 3, 2)  7.85 us

profile of v1, /device:TPU:0, one launch (start us, length us, event | category | flops | bytes accessed | tf_op | source)
XLA Modules:
  0.0 65.2 jit_solution(6203236072286788486)
XLA Ops:
  0.6 0.0 copy-start
  0.6 3.6 %copy.4 = f32[2,16,4096]{1,2,0:T(8,128)} copy(f32[2,16,4096]{2,1,0:T(8,128)} %param.2) | data formatting | bytes 1048576 | tf_op args[0]
  4.2 3.9 %copy.5 = f32[2,16,128,8,4]{2,3,4,0,1:T(8,128)S(1)} copy(f32[2,16,128,8,4]{1,4,3,2,0:T(4,128)} %bitcast.16) | data formatting | bytes 1048576 | tf_op jit(solution)/shard_map/reshape | solution.py:346
  8.1 0.0 copy-done
  8.1 2.6 %copy.6 = f32[2,16,4096]{1,2,0:T(8,128)} copy(f32[2,16,4096]{2,1,0:T(8,128)S(1)} %copy-done) | data formatting | bytes 1048576 | tf_op args[1]
  10.7 3.9 %copy.7 = f32[2,16,128,8,4]{2,3,4,0,1:T(8,128)S(1)} copy(f32[2,16,128,8,4]{1,4,3,2,0:T(4,128)} %bitcast.17) | data formatting | bytes 1048576 | tf_op jit(solution)/shard_map/reshape | solution.py:346
  14.7 0.1 pad_maximum_fusion.pq_ref
  14.8 34.7 %shard_map.41 = (f32[16,2,4,8,128]{4,3,2,1,0:T(8,128)S(1)}, f32[16,2,4,8,128]{4,3,2,1,0:T(8,128)S(1)}) custom-call(f32[16,2,2,4,8,128]{5,4,3,2,1,0:T(8,128)S(1)} %pad_maximum_fusion.pq_ref), custom_call_target="tpu_custom_call" | custom-call | tf_op jit(solution)/shard_map/pallas_call | solution.py:363
  49.4 4.4 %copy.9 = f32[2,16,128,8,4]{1,4,3,2,0:T(4,128)} copy(f32[2,16,128,8,4]{2,3,4,0,1:T(8,128)S(1)} %bitcast.13) | data formatting | bytes 1048576 | tf_op jit(solution)/shard_map/transpose | solution.py:351
  53.8 3.5 %copy.11 = f32[2,16,4096]{2,1,0:T(8,128)} copy(f32[2,16,4096]{1,2,0:T(8,128)} %bitcast.14) | data formatting | bytes 1048576
  57.3 4.4 %copy.8 = f32[2,16,128,8,4]{1,4,3,2,0:T(4,128)} copy(f32[2,16,128,8,4]{2,3,4,0,1:T(8,128)S(1)} %bitcast.12) | data formatting | bytes 1048576 | tf_op jit(solution)/shard_map/transpose | solution.py:351
  61.7 3.5 %copy.10 = f32[2,16,4096]{2,1,0:T(8,128)} copy(f32[2,16,4096]{1,2,0:T(8,128)} %bitcast.15) | data formatting | bytes 1048576
Async XLA Ops:
  0.6 7.5 %copy-start = (f32[2,16,4096]{2,1,0:T(8,128)S(1)}, f32[2,16,4096]{2,1,0:T(8,128)}, u32[]{:S(2)}) copy-start(f32[2,16,4096]{2,1,0:T(8,128)} %param.3) | copy-start | bytes 1572868

commit v2 on v1

--- a/solution.py
+++ b/solution.py
@@ -41,7 +41,37 @@
         body(r)
 
 
-def kernel(n, pq_ref, qn_ref, sn_ref, pq, b0, a0, c0, b1, a1, c1, b2, a2, c2, b3, a3, c3, b4, a4, c4, send, recv):
+def to_chunks(load4, store, xs, ts):
+    for a in range(32):
+        xs[pl.ds(4 * a, 4), :] = load4(a)
+    ts[...] = xs[...].T
+    lane = lax.broadcasted_iota(jnp.int32, (8, 128), 1) & 3
+    for u in range(4):
+        part = [ts[pl.ds(32 * c + u, 8, stride=4), :] for c in range(4)]
+        for q in range(4):
+            out = part[q]
+            for c in range(4):
+                if c != q:
+                    out = jnp.where(lane == c, pltpu.roll(part[c], (c - q) % 128, 1), out)
+            store(q, u, out)
+
+
+def from_chunks(load, store4, xs, ts):
+    lane = lax.broadcasted_iota(jnp.int32, (8, 128), 1) & 3
+    for u in range(4):
+        part = [load(q, u) for q in range(4)]
+        for c in range(4):
+            out = part[c]
+            for q in range(4):
+                if q != c:
+                    out = jnp.where(lane == q, pltpu.roll(part[q], (q - c) % 128, 1), out)
+            ts[pl.ds(32 * c + u, 8, stride=4), :] = out
+    xs[...] = ts[...].T
+    for a in range(32):
+        store4(a, xs[pl.ds(4 * a, 4), :])
+
+
+def kernel(n, p_in, q_in, qn_out, sn_out, xs, ts, qn_ref, sn_ref, pq, b0, a0, c0, b1, a1, c1, b2, a2, c2, b3, a3, c3, b4, a4, c4, send, recv):
     me = lax.axis_index("wide")
     sub = lax.broadcasted_iota(jnp.int32, (8, 128), 0)
     first = [sub < s for s in (1, 1, 1, 2, 4)]
@@ -136,7 +166,7 @@
                     other = jnp.where(odd, pltpu.roll(t[0], s, 0), pltpu.roll(t[0], 8 - s, 0))
                     coarse[at + i, k, 0] = 0.25 * (t[0] + other)
 
-        rows_loop(0, count, body, 2)
+        rows_loop(0, count, body, 2 if level == 0 else 5)
 
     def prolong(v, coarse, lo, hi, level, shift):
         def body(r):
@@ -193,8 +223,8 @@
 
     reach = min(REACH, n - 1)
     phase_a = [
-        put(1, pq_ref.at[pl.ds(12, 4)], pq.at[pl.ds(0, 4)]),
-        put(-1, pq_ref.at[pl.ds(0, 4)], pq.at[pl.ds(20, 4)]),
+        put(1, pq.at[pl.ds(16, 4)], pq.at[pl.ds(0, 4)]),
+        put(-1, pq.at[pl.ds(4, 4)], pq.at[pl.ds(20, 4)]),
     ]
     phase_b = [
         put(1, b1.at[pl.ds(8, 4)], b1.at[pl.ds(0, 4)]),
@@ -241,16 +271,42 @@
             def _():
                 pl.semaphore_signal(barrier, inc=1, device_id={"wide": me + d}, device_id_type=MESH)
 
+    def take(j):
+        def layer(k, carry):
+            for f, ref in enumerate((p_in, q_in)):
+
+                def load4(a):
+                    return ref[k, pl.ds(4 * j, 4), pl.ds(128 * a, 128)]
+
+                def store(q, u, x):
+                    pq[4 + 4 * j + q, f, k, u] = x
+
+                to_chunks(load4, store, xs.at[f], ts.at[f])
+            return carry
+
+        lax.fori_loop(0, 2, layer, 0)
+
+    def give(ref, out):
+        def layer(k, carry):
+            for j in range(4):
+
+                def load1(q, u):
+                    return ref[4 * j + q, k, u]
+
+                def store4(a, x):
+                    out[k, pl.ds(4 * j, 4), pl.ds(128 * a, 128)] = x
+
+                from_chunks(load1, store4, xs.at[j % 2], ts.at[j % 2])
+            return carry
+
+        lax.fori_loop(0, 2, layer, 0)
+
+    take(0)
+    take(3)
     pl.semaphore_wait(barrier, jnp.minimum(me, reach) + jnp.minimum(n - 1 - me, reach))
-
     start(phase_a)
-
-    def take(r):
-        for f in range(2):
-            for k, u in pairs:
-                pq[r + 4, f, k, u] = pq_ref[r, f, k, u]
-
-    rows_loop(0, 16, take, 2)
+    take(1)
+    take(2)
 
     def advance(lo, hi, own):
         def body(r):
@@ -299,79 +355,71 @@
     residual(c0, b0, b1, 4, 8, 4, 0)
 
     start(phase_b)
+    give(qn_ref, qn_out)
     arrive(phase_b)
     from_zero(a1, b1, 0, 16, 1)
-    sweep(a1, c1, b1, 1, 15, 1)
+    sweep(a1, c1, b1, 1, 15, 1, unroll=7)
     residual(c1, b1, b2, 4, 4, 5, 1)
 
     start(phase_c)
     arrive(phase_c)
     from_zero(a2, b2, 0, 14, 2)
-    sweep(a2, c2, b2, 1, 13, 2)
+    sweep(a2, c2, b2, 1, 13, 2, unroll=12)
     residual(c2, b2, b3, 5, 2, 20, 2)
 
     start(phase_d)
     arrive(phase_d)
     from_zero(a3, b3, 0, 42, 3)
-    sweep(a3, c3, b3, 1, 41, 3)
+    sweep(a3, c3, b3, 1, 41, 3, unroll=10)
     residual(c3, b3, b4, 2, 19, 0, 3)
 
     from_zero(a4, b4, 0, 19, 4)
     x, y = a4, c4
     for j in range(1, 8):
-        sweep(x, y, b4, j, 19 - j, 4)
+        sweep(x, y, b4, j, 19 - j, 4, unroll=20)
         x, y = y, x
 
     prolong(c3, x, 16, 26, 3, -2)
-    sweep(c3, a3, b3, 17, 25, 3)
-    sweep(a3, c3, b3, 18, 24, 3)
+    sweep(c3, a3, b3, 17, 25, 3, unroll=8)
+    sweep(a3, c3, b3, 18, 24, 3, unroll=8)
 
     prolong(c2, c3, 1, 13, 2, 35)
-    sweep(c2, a2, b2, 2, 12, 2)
-    sweep(a2, c2, b2, 3, 11, 2)
+    sweep(c2, a2, b2, 2, 12, 2, unroll=12)
+    sweep(a2, c2, b2, 3, 11, 2, unroll=12)
 
     prolong(c1, c2, 1, 15, 1, 6)
-    sweep(c1, a1, b1, 2, 14, 1)
-    sweep(a1, c1, b1, 3, 13, 1)
+    sweep(c1, a1, b1, 2, 14, 1, unroll=6)
+    sweep(a1, c1, b1, 3, 13, 1, unroll=5)
 
     prolong(c0, c1, 2, 22, 0, 4)
     sweep(c0, a0, b0, 3, 21, 0, unroll=2)
     sweep(a0, sn_ref, b0, 4, 20, 0, out=True, unroll=2)
 
+    give(sn_ref, sn_out)
     depart(range(len(copies)))
-
-
-def spread(x):
-    layers, rows, cols = x.shape
-    return x.reshape(layers, rows, 128, 8, 4).transpose(1, 0, 4, 3, 2)
-
-
-def gather(x):
-    rows, layers = x.shape[:2]
-    return x.transpose(1, 0, 4, 3, 2).reshape(layers, rows, 4096)
 
 
 def shards(stream_now, vorticity):
     n = lax.axis_size("wide")
-    pq = jnp.stack([spread(stream_now), spread(vorticity)], axis=1)
     vmem = pl.BlockSpec(memory_space=pltpu.VMEM)
-    shape = jax.ShapeDtypeStruct((ROWS, 2, 4, 8, 128), jnp.float32)
-    scratch = [pltpu.VMEM((EXT[0], 2, 2, 4, 8, 128), jnp.float32)]
+    shape = jax.ShapeDtypeStruct((2, ROWS, 4096), jnp.float32)
+    scratch = [pltpu.VMEM((2, 128, 128), jnp.float32)] * 2
+    scratch += [pltpu.VMEM((ROWS, 2, 4, 8, 128), jnp.float32)] * 2
+    scratch += [pltpu.VMEM((EXT[0], 2, 2, 4, 8, 128), jnp.float32)]
     for level in range(5):
         scratch += [pltpu.VMEM((EXT[level], 2, WIDTH[level], 8, 128), jnp.float32)] * 3
     count = 8 + 2 * min(REACH, n - 1)
-    qn, sn = pl.pallas_call(
+    return pl.pallas_call(
         functools.partial(kernel, n),
         out_shape=(shape, shape),
-        in_specs=[vmem],
+        in_specs=[vmem, vmem],
         out_specs=(vmem, vmem),
         scratch_shapes=scratch
         + [pltpu.SemaphoreType.DMA((count,)), pltpu.SemaphoreType.DMA((count,))],
         compiler_params=pltpu.CompilerParams(
             collective_id=0, has_side_effects=True, vmem_limit_bytes=40 * 1024 * 1024
         ),
-    )(pq)
-    return gather(qn), gather(sn)
+    )(stream_now, vorticity)
 
 
 def solution(mesh):

time: 65.3 us -> 37 us (0.57)
  local copies, waits for them, and re-layouts: 29.7 us -> 3.66 us
  Pallas kernels: 34.7 us -> 32.2 us
    unnamed x6, local copies, waits for them, and re-layouts: 13.2 us -> 3.66 us
    transpose x2 -> x0, local copies, waits for them, and re-layouts: 8.71 us -> none  [gather(): return x.transpose(1, 0, 4, 3, 2).reshape(layers, rows, 4096)]
    reshape x2 -> x0, local copies, waits for them, and re-layouts: 7.85 us -> none  [spread(): return x.reshape(layers, rows, 128, 8, 4).transpose(1, 0, 4, 3, 2)]
    pallas_call x1, Pallas kernels: 34.7 us -> 32.2 us  [shards(): pl.pallas_call(functools.partial(kernel, n), out_shape=(shape, shape), in...]
where the time goes in v2:
time: 37 us; the launch traced here: 36.5 us
  Pallas kernels  32.2 us (87%)
  local copies, waits for them, and re-layouts  3.66 us (10%)
  between operations  0.65 us (2%)
    pallas_call x1, Pallas kernels, shards(): pl.pallas_call(functools.partial(kernel, n), out_shape=(shape, shape), in...  32.2 us
    unnamed x6, local copies, waits for them, and re-layouts  3.66 us

profile of v2, /device:TPU:0, one launch (start us, length us, event | category | flops | bytes accessed | tf_op | source)
XLA Modules:
  0.0 36.5 jit_solution(8483197062947789584)
XLA Ops:
  0.6 0.0 copy-start
  0.6 1.0 %copy-done = f32[2,16,4096]{2,1,0:T(8,128)S(1)} copy-done((f32[2,16,4096]{2,1,0:T(8,128)S(1)}, f32[2,16,4096]{2,1,0:T(8,128)}, u32[]{:S(2)}) %copy-start) | copy-done | bytes 524312
  1.7 0.0 copy-start.1
  1.7 1.0 %copy-done.1 = f32[2,16,4096]{2,1,0:T(8,128)S(1)} copy-done((f32[2,16,4096]{2,1,0:T(8,128)S(1)}, f32[2,16,4096]{2,1,0:T(8,128)}, u32[]{:S(2)}) %copy-start.1) | copy-done | bytes 524312
  2.7 32.2 %shard_map.41 = (f32[2,16,4096]{2,1,0:T(8,128)S(1)}, f32[2,16,4096]{2,1,0:T(8,128)S(1)}) custom-call(f32[2,16,4096]{2,1,0:T(8,128)S(1)} %copy-done, f32[2,16,4096]{2,1,0:T(8,128)S(1)} %copy-done.1), custom_call_target="tpu_custom_call" | custom-call | tf_op jit(solution)/shard_map/pallas_call | solution.py:412
  34.9 0.8 %copy.6 = f32[2,16,4096]{2,1,0:T(8,128)} copy(f32[2,16,4096]{2,1,0:T(8,128)S(1)} %get-tuple-element.4) | data formatting | bytes 1048576
  35.7 0.8 %copy.7 = f32[2,16,4096]{2,1,0:T(8,128)} copy(f32[2,16,4096]{2,1,0:T(8,128)S(1)} %get-tuple-element.5) | data formatting | bytes 1048576
Async XLA Ops:
  0.6 1.0 %copy-start = (f32[2,16,4096]{2,1,0:T(8,128)S(1)}, f32[2,16,4096]{2,1,0:T(8,128)}, u32[]{:S(2)}) copy-start(f32[2,16,4096]{2,1,0:T(8,128)} %p_in.1) | copy-start | bytes 1572868
  1.7 1.0 %copy-start.1 = (f32[2,16,4096]{2,1,0:T(8,128)S(1)}, f32[2,16,4096]{2,1,0:T(8,128)}, u32[]{:S(2)}) copy-start(f32[2,16,4096]{2,1,0:T(8,128)} %q_in.1) | copy-start | bytes 1572868

commit v3 on v2

--- a/solution.py
+++ b/solution.py
@@ -71,7 +71,7 @@
         store4(a, xs[pl.ds(4 * a, 4), :])
 
 
-def kernel(n, p_in, q_in, qn_out, sn_out, xs, ts, qn_ref, sn_ref, pq, b0, a0, c0, b1, a1, c1, b2, a2, c2, b3, a3, c3, b4, a4, c4, send, recv):
+def kernel(n, p_in, q_in, qn_out, sn_out, xs, ts, qn_ref, sn_ref, pq, b0, a0, c0, b1, a1, c1, b2, a2, c2, b3, a3, c3, b4, a4, c4, g3, send, recv):
     me = lax.axis_index("wide")
     sub = lax.broadcasted_iota(jnp.int32, (8, 128), 0)
     first = [sub < s for s in (1, 1, 1, 2, 4)]
@@ -166,7 +166,7 @@
                     other = jnp.where(odd, pltpu.roll(t[0], s, 0), pltpu.roll(t[0], 8 - s, 0))
                     coarse[at + i, k, 0] = 0.25 * (t[0] + other)
 
-        rows_loop(0, count, body, 2 if level == 0 else 5)
+        rows_loop(0, count, body, 4 if level == 0 else 5)
 
     def prolong(v, coarse, lo, hi, level, shift):
         def body(r):
@@ -223,8 +223,8 @@
 
     reach = min(REACH, n - 1)
     phase_a = [
-        put(1, pq.at[pl.ds(16, 4)], pq.at[pl.ds(0, 4)]),
-        put(-1, pq.at[pl.ds(4, 4)], pq.at[pl.ds(20, 4)]),
+        put(1, pq.at[pl.ds(17, 3)], pq.at[pl.ds(1, 3)]),
+        put(-1, pq.at[pl.ds(4, 3)], pq.at[pl.ds(20, 3)]),
     ]
     phase_b = [
         put(1, b1.at[pl.ds(8, 4)], b1.at[pl.ds(0, 4)]),
@@ -236,10 +236,14 @@
         put(2, b2.at[pl.ds(8, 1)], b2.at[pl.ds(0, 1)]),
         put(-2, b2.at[pl.ds(5, 1)], b2.at[pl.ds(13, 1)]),
     ]
+    phase_e = [
+        put(1, c0.at[pl.ds(18, 1)], c0.at[pl.ds(2, 1)]),
+        put(-1, c0.at[pl.ds(5, 1)], c0.at[pl.ds(21, 1)]),
+    ]
     phase_d = []
     for d in range(reach, 0, -1):
         for signed in (d, -d):
-            phase_d.append(put(signed, b3.at[pl.ds(20, 2)], b3.at[pl.ds(20 - 2 * signed, 2)]))
+            phase_d.append(put(signed, g3.at[pl.ds(10, 1)], g3.at[pl.ds(10 - signed, 1)]))
 
     def clear(ref, lo, hi, inner):
         for r in range(lo, hi):
@@ -250,18 +254,20 @@
 
     @pl.when(me == 0)
     def _():
-        clear(pq, 0, 4, [(f, k, u) for f in range(2) for k, u in pairs])
+        clear(pq, 1, 4, [(f, k, u) for f in range(2) for k, u in pairs])
+        clear(c0, 2, 3, pairs)
 
     @pl.when(me == n - 1)
     def _():
-        clear(pq, 20, 24, [(f, k, u) for f in range(2) for k, u in pairs])
+        clear(pq, 20, 23, [(f, k, u) for f in range(2) for k, u in pairs])
+        clear(c0, 21, 22, pairs)
 
     clear(b1, 0, 4, [(k, u) for k in range(2) for u in range(2)])
     clear(b1, 12, 16, [(k, u) for k in range(2) for u in range(2)])
     clear(b2, 0, 5, [(0, 0), (1, 0)])
     clear(b2, 9, 14, [(0, 0), (1, 0)])
-    clear(b3, 0, 20, [(0, 0), (1, 0)])
-    clear(b3, 22, 42, [(0, 0), (1, 0)])
+    clear(g3, 0, 10, [(0,), (1,)])
+    clear(g3, 11, 21, [(0,), (1,)])
 
     barrier = pltpu.get_barrier_semaphore()
     for d in range(-reach, reach + 1):
@@ -286,20 +292,16 @@
 
         lax.fori_loop(0, 2, layer, 0)
 
-    def give(ref, out):
-        def layer(k, carry):
-            for j in range(4):
-
-                def load1(q, u):
-                    return ref[4 * j + q, k, u]
-
-                def store4(a, x):
-                    out[k, pl.ds(4 * j, 4), pl.ds(128 * a, 128)] = x
-
-                from_chunks(load1, store4, xs.at[j % 2], ts.at[j % 2])
-            return carry
-
-        lax.fori_loop(0, 2, layer, 0)
+    def give(ref, out, k, js):
+        for j in js:
+
+            def load1(q, u):
+                return ref[4 * j + q, k, u]
+
+            def store4(a, x):
+                out[k, pl.ds(4 * j, 4), pl.ds(128 * a, 128)] = x
+
+            from_chunks(load1, store4, xs.at[j % 2], ts.at[j % 2])
 
     take(0)
     take(3)
@@ -341,34 +343,47 @@
                     if own:
                         qn_ref[r - 4, k, u] = qc - change
 
-        rows_loop(lo, hi, body, 1)
+        rows_loop(lo, hi, body, 2)
 
     advance(5, 19, True)
     arrive(phase_a)
-    advance(1, 4, False)
+    advance(2, 4, False)
     advance(4, 5, True)
     advance(19, 20, True)
-    advance(20, 23, False)
-
-    sweep(pq, a0, b0, 1, 23, 0, load_p, unroll=2)
-    sweep(a0, c0, b0, 2, 22, 0, unroll=2)
+    advance(20, 22, False)
+
+    sweep(pq, a0, b0, 2, 22, 0, load_p, unroll=4)
+    sweep(a0, c0, b0, 3, 21, 0, unroll=4)
     residual(c0, b0, b1, 4, 8, 4, 0)
 
     start(phase_b)
-    give(qn_ref, qn_out)
+    start(phase_e)
+    give(qn_ref, qn_out, 0, range(4))
     arrive(phase_b)
     from_zero(a1, b1, 0, 16, 1)
     sweep(a1, c1, b1, 1, 15, 1, unroll=7)
     residual(c1, b1, b2, 4, 4, 5, 1)
 
     start(phase_c)
+    give(qn_ref, qn_out, 1, (0, 1))
     arrive(phase_c)
     from_zero(a2, b2, 0, 14, 2)
     sweep(a2, c2, b2, 1, 13, 2, unroll=12)
     residual(c2, b2, b3, 5, 2, 20, 2)
 
+    for k in range(2):
+        g3[10, k] = jnp.where(odd1, b3[21, k, 0], b3[20, k, 0])
     start(phase_d)
+    give(qn_ref, qn_out, 1, (2, 3))
     arrive(phase_d)
+
+    def unpack(i):
+        for k in range(2):
+            z = g3[i, k]
+            b3[2 * i, k, 0] = jnp.where(odd1, pltpu.roll(z, 1, 0), z)
+            b3[2 * i + 1, k, 0] = jnp.where(odd1, z, pltpu.roll(z, 7, 0))
+
+    rows_loop(0, 21, unpack, 7)
     from_zero(a3, b3, 0, 42, 3)
     sweep(a3, c3, b3, 1, 41, 3, unroll=10)
     residual(c3, b3, b4, 2, 19, 0, 3)
@@ -391,12 +406,15 @@
     sweep(c1, a1, b1, 2, 14, 1, unroll=6)
     sweep(a1, c1, b1, 3, 13, 1, unroll=5)
 
+    arrive(phase_e)
+    depart(phase_e)
     prolong(c0, c1, 2, 22, 0, 4)
-    sweep(c0, a0, b0, 3, 21, 0, unroll=2)
-    sweep(a0, sn_ref, b0, 4, 20, 0, out=True, unroll=2)
-
-    give(sn_ref, sn_out)
-    depart(range(len(copies)))
+    sweep(c0, a0, b0, 3, 21, 0, unroll=4)
+    sweep(a0, sn_ref, b0, 4, 20, 0, out=True, unroll=4)
+
+    for k in range(2):
+        give(sn_ref, sn_out, k, range(4))
+    depart(phase_a + phase_b + phase_c + phase_d)
 
 
 def shards(stream_now, vorticity):
@@ -408,13 +426,14 @@
     scratch += [pltpu.VMEM((EXT[0], 2, 2, 4, 8, 128), jnp.float32)]
     for level in range(5):
         scratch += [pltpu.VMEM((EXT[level], 2, WIDTH[level], 8, 128), jnp.float32)] * 3
-    count = 8 + 2 * min(REACH, n - 1)
+    count = 10 + 2 * min(REACH, n - 1)
     return pl.pallas_call(
         functools.partial(kernel, n),
         out_shape=(shape, shape),
         in_specs=[vmem, vmem],
         out_specs=(vmem, vmem),
         scratch_shapes=scratch
+        + [pltpu.VMEM((2 * REACH + 1, 2, 8, 128), jnp.float32)]
         + [pltpu.SemaphoreType.DMA((count,)), pltpu.SemaphoreType.DMA((count,))],
         compiler_params=pltpu.CompilerParams(
             collective_id=0, has_side_effects=True, vmem_limit_bytes=40 * 1024 * 1024

time: 37 us -> 32.5 us (0.88)
  Pallas kernels: 32.2 us -> 27.9 us
    pallas_call x1, Pallas kernels: 32.2 us -> 27.9 us  [shards(): pl.pallas_call(functools.partial(kernel, n), out_shape=(shape, shape), in...]
where the time goes in v3:
time: 32.5 us; the launch traced here: 32.3 us
  Pallas kernels  27.9 us (86%)
  local copies, waits for them, and re-layouts  3.66 us (11%)
  between operations  0.65 us (2%)
    pallas_call x1, Pallas kernels, shards(): pl.pallas_call(functools.partial(kernel, n), out_shape=(shape, shape), in...  27.9 us
    unnamed x6, local copies, waits for them, and re-layouts  3.66 us

profile of v3, /device:TPU:0, one launch (start us, length us, event | category | flops | bytes accessed | tf_op | source)
XLA Modules:
  0.0 32.3 jit_solution(2977080561735606439)
XLA Ops:
  0.6 0.0 copy-start
  0.6 1.0 %copy-done = f32[2,16,4096]{2,1,0:T(8,128)S(1)} copy-done((f32[2,16,4096]{2,1,0:T(8,128)S(1)}, f32[2,16,4096]{2,1,0:T(8,128)}, u32[]{:S(2)}) %copy-start) | copy-done | bytes 524312
  1.7 0.0 copy-start.1
  1.7 1.0 %copy-done.1 = f32[2,16,4096]{2,1,0:T(8,128)S(1)} copy-done((f32[2,16,4096]{2,1,0:T(8,128)S(1)}, f32[2,16,4096]{2,1,0:T(8,128)}, u32[]{:S(2)}) %copy-start.1) | copy-done | bytes 524312
  2.7 27.9 %shard_map.41 = (f32[2,16,4096]{2,1,0:T(8,128)S(1)}, f32[2,16,4096]{2,1,0:T(8,128)S(1)}) custom-call(f32[2,16,4096]{2,1,0:T(8,128)S(1)} %copy-done, f32[2,16,4096]{2,1,0:T(8,128)S(1)} %copy-done.1), custom_call_target="tpu_custom_call" | custom-call | tf_op jit(solution)/shard_map/pallas_call | solution.py:430
  30.7 0.8 %copy.6 = f32[2,16,4096]{2,1,0:T(8,128)} copy(f32[2,16,4096]{2,1,0:T(8,128)S(1)} %get-tuple-element.4) | data formatting | bytes 1048576
  31.5 0.8 %copy.7 = f32[2,16,4096]{2,1,0:T(8,128)} copy(f32[2,16,4096]{2,1,0:T(8,128)S(1)} %get-tuple-element.5) | data formatting | bytes 1048576
Async XLA Ops:
  0.6 1.0 %copy-start = (f32[2,16,4096]{2,1,0:T(8,128)S(1)}, f32[2,16,4096]{2,1,0:T(8,128)}, u32[]{:S(2)}) copy-start(f32[2,16,4096]{2,1,0:T(8,128)} %p_in.1) | copy-start | bytes 1572868
  1.7 1.0 %copy-start.1 = (f32[2,16,4096]{2,1,0:T(8,128)S(1)}, f32[2,16,4096]{2,1,0:T(8,128)}, u32[]{:S(2)}) copy-start(f32[2,16,4096]{2,1,0:T(8,128)} %q_in.1) | copy-start | bytes 1572868

commit v4 on v3

--- a/solution.py
+++ b/solution.py
@@ -71,7 +71,13 @@
         store4(a, xs[pl.ds(4 * a, 4), :])
 
 
-def kernel(n, p_in, q_in, qn_out, sn_out, xs, ts, qn_ref, sn_ref, pq, b0, a0, c0, b1, a1, c1, b2, a2, c2, b3, a3, c3, b4, a4, c4, g3, send, recv):
+def kernel(n, p_hbm, q_hbm, qn_out, sn_out, xs, ts, qn_ref, sn_ref, pq, b0, a0, c0, b1, a1, c1, b2, a2, c2, b3, a3, c3, b4, a4, c4, g3, p_in, q_in, fetch, send, recv):
+    fetches = [
+        pltpu.make_async_copy(p_hbm, p_in, fetch.at[0]),
+        pltpu.make_async_copy(q_hbm, q_in, fetch.at[1]),
+    ]
+    for f in fetches:
+        f.start()
     me = lax.axis_index("wide")
     sub = lax.broadcasted_iota(jnp.int32, (8, 128), 0)
     first = [sub < s for s in (1, 1, 1, 2, 4)]
@@ -303,6 +309,8 @@
 
             from_chunks(load1, store4, xs.at[j % 2], ts.at[j % 2])
 
+    for f in fetches:
+        f.wait()
     take(0)
     take(3)
     pl.semaphore_wait(barrier, jnp.minimum(me, reach) + jnp.minimum(n - 1 - me, reach))
@@ -430,10 +438,12 @@
     return pl.pallas_call(
         functools.partial(kernel, n),
         out_shape=(shape, shape),
-        in_specs=[vmem, vmem],
+        in_specs=[pl.BlockSpec(memory_space=pltpu.HBM)] * 2,
         out_specs=(vmem, vmem),
         scratch_shapes=scratch
         + [pltpu.VMEM((2 * REACH + 1, 2, 8, 128), jnp.float32)]
+        + [pltpu.VMEM((2, ROWS, 4096), jnp.float32)] * 2
+        + [pltpu.SemaphoreType.DMA((2,))]
         + [pltpu.SemaphoreType.DMA((count,)), pltpu.SemaphoreType.DMA((count,))],
         compiler_params=pltpu.CompilerParams(
             collective_id=0, has_side_effects=True, vmem_limit_bytes=40 * 1024 * 1024

time: 32.5 us -> 32.6 us (level)
  no operation moved by 1% of the time
where the time goes in v4:
time: 32.6 us; the launch traced here: 32.4 us
  Pallas kernels  28 us (86%)
  local copies, waits for them, and re-layouts  3.66 us (11%)
  between operations  0.65 us (2%)
    pallas_call x1, Pallas kernels, shards(): pl.pallas_call(functools.partial(kernel, n), out_shape=(shape, shape), in...  28 us
    unnamed x6, local copies, waits for them, and re-layouts  3.66 us

profile of v4, /device:TPU:0, one launch (start us, length us, event | category | flops | bytes accessed | tf_op | source)
XLA Modules:
  0.0 32.4 jit_solution(10266547236488622938)
XLA Ops:
  0.6 0.0 copy-start
  0.6 1.0 %copy-done = f32[2,16,4096]{2,1,0:T(8,128)S(1)} copy-done((f32[2,16,4096]{2,1,0:T(8,128)S(1)}, f32[2,16,4096]{2,1,0:T(8,128)}, u32[]{:S(2)}) %copy-start) | copy-done | bytes 524312
  1.7 0.0 copy-start.1
  1.7 1.0 %copy-done.1 = f32[2,16,4096]{2,1,0:T(8,128)S(1)} copy-done((f32[2,16,4096]{2,1,0:T(8,128)S(1)}, f32[2,16,4096]{2,1,0:T(8,128)}, u32[]{:S(2)}) %copy-start.1) | copy-done | bytes 524312
  2.7 28.0 %shard_map.41 = (f32[2,16,4096]{2,1,0:T(8,128)S(1)}, f32[2,16,4096]{2,1,0:T(8,128)S(1)}) custom-call(f32[2,16,4096]{2,1,0:T(8,128)S(1)} %copy-done, f32[2,16,4096]{2,1,0:T(8,128)S(1)} %copy-done.1), custom_call_target="tpu_custom_call" | custom-call | tf_op jit(solution)/shard_map/pallas_call | solution.py:438
  30.8 0.8 %copy.6 = f32[2,16,4096]{2,1,0:T(8,128)} copy(f32[2,16,4096]{2,1,0:T(8,128)S(1)} %get-tuple-element.4) | data formatting | bytes 1048576
  31.6 0.8 %copy.7 = f32[2,16,4096]{2,1,0:T(8,128)} copy(f32[2,16,4096]{2,1,0:T(8,128)S(1)} %get-tuple-element.5) | data formatting | bytes 1048576
Async XLA Ops:
  0.6 1.0 %copy-start = (f32[2,16,4096]{2,1,0:T(8,128)S(1)}, f32[2,16,4096]{2,1,0:T(8,128)}, u32[]{:S(2)}) copy-start(f32[2,16,4096]{2,1,0:T(8,128)} %p_hbm.1) | copy-start | bytes 1572868
  1.7 1.0 %copy-start.1 = (f32[2,16,4096]{2,1,0:T(8,128)S(1)}, f32[2,16,4096]{2,1,0:T(8,128)}, u32[]{:S(2)}) copy-start(f32[2,16,4096]{2,1,0:T(8,128)} %q_hbm.1) | copy-start | bytes 1572868
